TPU v7x, 128 devices: a whole 4x4x4 slice. The times are simulated.
128 devices in a mesh: row: 32 (over x, y, core), col: 4 (over z).
Axes of the slice: x: 4, y: 4, z: 4, core: 2. Of those that a mesh axis runs over, the one named last changes fastest.
Arguments:
- trailing: float32 [4096, 4096], P('row'), as said below
- inverse_rows: float32 [4096, 512], P('row')
- rhs_tail: float32 [4096, 2048], P('row', 'col'), may hold values from -6 to 6
- coupling: float32 [32768, 4096], P('row', 'col'), may hold values from -0.09375 to 0.09375
- rhs_head: float32 [32768, 2048], P('row', 'col'), may hold values from -6 to 6
- child_rows: int32 [64, 256], replicated, may hold values from 0 to 4095, as said below
- owner: int32 [64], replicated, may hold values from 0 to 31, as said below
Outputs:
- remaining: float32 [32768, 2048], P('row', 'col')
- solved: float32 [4096, 2048], P(None, 'col')
- handed: float32 [128, 256, 2048], P('row', None, 'col')
Inputs may be any that keep to these rules, and one draw needn't show every extreme that they name: `trailing`: blocks of 512 x 512 on or below the block diagonal are zero. `child_rows`: each list holds 256 distinct rows in increasing order. `owner`: one subtree group owns exactly 4 child blocks, two groups own exactly one each, every other group owns two.
All inputs are finite; a program needn't handle non-finite values.
Results may differ from a plain program's by a relative error of at most 0.0001.
Values sent between devices are 32-bit elements; how exact they have to be, the bound alone decides.
No kernel may reach another device: no remote copies, remote signals or barrier semaphores. Data moves between devices by JAX's collectives and lax.ppermute only.
A program may use at most 128 MiB of HBM per device.

v0:
```python
import functools

import jax
import jax.numpy as jnp
from jax import lax
from jax.experimental import pallas as pl
from jax.experimental.pallas import tpu as pltpu
from jax.sharding import Mesh, PartitionSpec as P

SLOTS = 4
NX, NY, NC = 4, 4, 2
ROW = ("x", "y", "core")
SWAP = [(0, 1), (1, 0)]
MIB = 1024 * 1024

def three_terms(a):
    top = a.astype(jnp.bfloat16)
    rest = a - top.astype(jnp.float32)
    mid = rest.astype(jnp.bfloat16)
    return top, mid, (rest - mid.astype(jnp.float32)).astype(jnp.bfloat16)


def mm(a, b, a_axis=1):
    n = b.shape[1]
    top, mid, low = three_terms(a)
    terms = jnp.concatenate(three_terms(b), axis=1)

    def dot(u, v):
        return lax.dot_general(u, v, (((a_axis,), (0,)), ((), ())), preferred_element_type=jnp.float32)

    first = dot(top, terms)
    second = dot(mid, terms[:, : 2 * n])
    third = dot(low, terms[:, :n])
    small = first[:, 2 * n :] + second[:, n:] + third
    return first[:, :n] + ((first[:, n : 2 * n] + second[:, :n]) + small)


def mm_t(a, b):
    return mm(a, b, 0)


def split(a):
    top = a.astype(jnp.bfloat16)
    return top, (a - top.astype(jnp.float32)).astype(jnp.bfloat16)


def mm3(a_top, a_low, b_top, b_low):
    one = functools.partial(jnp.dot, preferred_element_type=jnp.float32)
    return one(a_top, b_top) + (one(a_low, b_top) + one(a_top, b_low))


def both_cores(own):
    return lax.ppermute(own, "core", SWAP)


ONE, THREE = [[(i, i ^ s) for i in range(NY)] for s in (1, 3)]


def neighbours_y(piece):
    return lax.ppermute(piece, "y", ONE), lax.ppermute(piece, "y", THREE)


def pass_on_y(a, b, axis):
    n = a.shape[axis] // 2
    c = lax.ppermute(lax.slice_in_dim(b, 0, n, axis=axis), "y", ONE)
    d = lax.ppermute(lax.slice_in_dim(a, n, 2 * n, axis=axis), "y", THREE)
    return a, b, c, d


def exchange_y(piece, axis=0):
    return pass_on_y(*neighbours_y(piece), axis)


def solve_kernel(p, idx, fac_own, fac_other, r_own, r_other, out, g_hi, t_mid, g_low, sems):
    @pl.when(idx[0] == p)
    def _():
        width = g_hi.shape[-1]
        copies = []
        for n, (dst, y0, col) in enumerate(((g_hi, 2, 0), (t_mid, 0, width), (g_low, 0, 0))):
            for j, fac in enumerate((fac_own, fac_other)):
                src = fac.at[pl.ds(y0, 2), :, pl.ds(col, width)]
                cp = pltpu.make_async_copy(src, dst.at[j], sems.at[2 * n + j])
                cp.start()
                copies.append(cp)

        def rows(y0):
            a = r_own[pl.ds(y0, 2)]
            b = r_other[pl.ds(y0, 2)]
            return jnp.concatenate([a.reshape(-1, a.shape[-1]), b.reshape(-1, b.shape[-1])], axis=0)

        r_hi, r_low = rows(2), rows(0)
        copies[0].wait()
        copies[1].wait()
        x_hi = mm_t(g_hi[...].reshape(width, width), r_hi)
        copies[2].wait()
        copies[3].wait()
        r_low = r_low - mm(t_mid[...].reshape(width, width), x_hi)
        copies[4].wait()
        copies[5].wait()
        x_low = mm_t(g_low[...].reshape(width, width), r_low)
        out[...] = jnp.where(idx[2] == 0, x_low, x_hi)


def solve(p, idx, packed, packed_other, r_own, r_other, width):
    part = r_own.shape[-1]
    vmem = pl.BlockSpec(memory_space=pltpu.VMEM)
    hbm = pl.BlockSpec(memory_space=pltpu.HBM)
    half = pltpu.VMEM((2, 2, width // 4, width), jnp.float32)
    return pl.pallas_call(
        functools.partial(solve_kernel, p),
        out_shape=jax.ShapeDtypeStruct((width, part), jnp.float32),
        in_specs=[pl.BlockSpec(memory_space=pltpu.SMEM), hbm, hbm, vmem, vmem],
        out_specs=vmem,
        scratch_shapes=[half, half, half, pltpu.SemaphoreType.DMA((6,))],
        compiler_params=pltpu.CompilerParams(vmem_limit_bytes=24 * MIB),
        cost_estimate=pl.CostEstimate(flops=1000, bytes_accessed=1000, transcendentals=0),
        name="solve_pair",
    )(idx, packed, packed_other, r_own, r_other)


def update_kernel(p, idx, mine, other, r_own, trailing, near, far, top, bottom, out, t_buf, sems):
    x, y, core = idx[0], idx[1], idx[2]
    ny, rows, pair = t_buf.shape
    half = rows // 2
    moves = (
        (trailing.at[:, pl.ds(p * pair, pair)], t_buf.at[y]),
        (near, t_buf.at[y ^ 1]),
        (far, t_buf.at[y ^ 3]),
        (top, t_buf.at[y ^ 2, pl.ds(0, half)]),
        (bottom, t_buf.at[y ^ 2, pl.ds(half, half)]),
    )

    @pl.when(x >= p)
    def _():
        out[...] = r_own[...]

    @pl.when(x < p)
    def _():
        copies = [pltpu.make_async_copy(src, dst, sems.at[n]) for n, (src, dst) in enumerate(moves)]
        for cp in copies:
            cp.start()
        first = jnp.where(core == 0, mine[...], other[...])
        second = jnp.where(core == 0, other[...], mine[...])
        block = jnp.concatenate([first, second], axis=0)
        for cp in copies:
            cp.wait()
        step = mm(t_buf[...].reshape(ny * rows, pair), block).reshape(r_own.shape)
        out[...] = r_own[...] - step


def update(p, idx, mine, other, r_own, trailing, pieces):
    vmem = pl.BlockSpec(memory_space=pltpu.VMEM)
    hbm = pl.BlockSpec(memory_space=pltpu.HBM)
    rows, pair = pieces[0].shape
    return pl.pallas_call(
        functools.partial(update_kernel, p),
        out_shape=jax.ShapeDtypeStruct(r_own.shape, jnp.float32),
        in_specs=[pl.BlockSpec(memory_space=pltpu.SMEM), vmem, vmem, vmem] + [hbm] * 5,
        out_specs=vmem,
        scratch_shapes=[pltpu.VMEM((NY, rows, pair), jnp.float32), pltpu.SemaphoreType.DMA((5,))],
        compiler_params=pltpu.CompilerParams(vmem_limit_bytes=24 * MIB),
        cost_estimate=pl.CostEstimate(flops=1000, bytes_accessed=1000, transcendentals=0),
        name="update_rows",
    )(idx, mine, other, r_own, trailing, *pieces)


def join_kernel(idx, own, near, far, top, bottom, out, sems):
    y = idx[1]
    height, part = own.shape[1:]
    half = height // 2

    def columns(s):
        return pl.ds(pl.multiple_of((y ^ s) * part, part), part)

    moves = (
        (own, out.at[:, :, columns(0)]),
        (near, out.at[:, :, columns(1)]),
        (far, out.at[:, :, columns(3)]),
        (top, out.at[:, pl.ds(0, half), columns(2)]),
        (bottom, out.at[:, pl.ds(half, half), columns(2)]),
    )
    copies = [pltpu.make_async_copy(src, dst, sems.at[n]) for n, (src, dst) in enumerate(moves)]
    for cp in copies:
        cp.start()
    for cp in copies:
        cp.wait()


def join(idx, own, pieces):
    n, height, part = own.shape
    hbm = pl.BlockSpec(memory_space=pltpu.HBM)
    return pl.pallas_call(
        join_kernel,
        grid=(1,),
        out_shape=jax.ShapeDtypeStruct((n, height, NY * part), jnp.float32),
        in_specs=[pl.BlockSpec(memory_space=pltpu.SMEM)] + [hbm] * 5,
        out_specs=pl.BlockSpec((n, height, NY * part), lambda i: (0, 0, 0)),
        scratch_shapes=[pltpu.SemaphoreType.DMA((5,))],
        compiler_params=pltpu.CompilerParams(vmem_limit_bytes=24 * MIB),
        cost_estimate=pl.CostEstimate(flops=0, bytes_accessed=n * 3 * MIB, transcendentals=0),
        name="join_columns",
    )(idx, own, *pieces)


def assemble_kernel(idx, own, other, *refs):
    core = idx[2]
    out, top, low = refs[-3:]
    height = own.shape[1]
    for panel in range(2):
        value = jnp.where(core == panel, own[0], other[0])
        rows = pl.ds(panel * height, height)
        out[rows] = value
        top[0, rows], low[0, rows] = split(value)


def assemble(idx, first, own, other, solved):
    n, height, columns = own.shape
    hbm = pl.BlockSpec(memory_space=pltpu.HBM)
    block = pl.BlockSpec((1, height, columns), lambda i: (i, 0, 0))
    terms = pl.BlockSpec((1, 2 * height, columns), lambda i: (i, 0, 0))
    term = jax.ShapeDtypeStruct((n, 2 * height, columns), jnp.bfloat16)
    return pl.pallas_call(
        assemble_kernel,
        grid=(n,),
        out_shape=[jax.ShapeDtypeStruct((NX * 2 * height, columns), jnp.float32), term, term],
        in_specs=[pl.BlockSpec(memory_space=pltpu.SMEM), block, block] + [hbm] * len(solved),
        out_specs=[pl.BlockSpec((2 * height, columns), lambda i: (first + i, 0)), terms, terms],
        input_output_aliases={3: 0} if solved else {},
        compiler_params=pltpu.CompilerParams(vmem_limit_bytes=32 * MIB),
        cost_estimate=pl.CostEstimate(flops=0, bytes_accessed=n * 6 * MIB, transcendentals=0),
        name="assemble_pairs",
    )(idx, own, other, *solved)


def product_kernel(start, c, b_top, b_low, out):
    @pl.when(pl.program_id(1) == 0)
    def _():
        out[...] = start[...]

    a_top, a_low = split(c[0])
    out[...] -= mm3(a_top, a_low, b_top[0], b_low[0])


def product(start, blocks, top, low, first):
    rows, columns = start.shape
    count, pair, _ = top.shape
    tile = rows // (4 if count == 1 else 2)
    whole = pl.BlockSpec((tile, columns), lambda i, j: (i, 0))
    term = pl.BlockSpec((1, pair, columns), lambda i, j: (j, 0, 0))
    return pl.pallas_call(
        product_kernel,
        grid=(rows // tile, count),
        out_shape=jax.ShapeDtypeStruct(start.shape, jnp.float32),
        in_specs=[whole, pl.BlockSpec((1, tile, pair), lambda i, j: (first + j, i, 0)), term, term],
        out_specs=whole,
        compiler_params=pltpu.CompilerParams(vmem_limit_bytes=40 * MIB),
        cost_estimate=pl.CostEstimate(
            flops=6 * rows * pair * columns * count, bytes_accessed=count * 8 * MIB, transcendentals=0
        ),
        name="product",
    )(start, blocks, top, low)


def hand_kernel(filled, taken, solved, out):
    slot = pl.program_id(0)
    count = out.shape[1]

    @pl.when(filled[slot] == 1)
    def _():
        def body(n, carry):
            for u in range(8):
                i = n * 8 + u
                out[0, pl.ds(i, 1)] = solved[pl.ds(taken[slot, i], 1)]
            return carry

        lax.fori_loop(0, count // 8, body, 0)

    @pl.when(filled[slot] == 0)
    def _():
        out[...] = jnp.zeros_like(out)


def hand(filled, taken, solved):
    slots, count = taken.shape
    columns = solved.shape[1]
    smem = pl.BlockSpec(memory_space=pltpu.SMEM)
    return pl.pallas_call(
        hand_kernel,
        grid=(slots,),
        out_shape=jax.ShapeDtypeStruct((slots, count, columns), jnp.float32),
        in_specs=[smem, smem, pl.BlockSpec(solved.shape, lambda i: (0, 0))],
        out_specs=pl.BlockSpec((1, count, columns), lambda i: (i, 0, 0)),
        compiler_params=pltpu.CompilerParams(vmem_limit_bytes=32 * MIB),
        cost_estimate=pl.CostEstimate(flops=0, bytes_accessed=10 * MIB, transcendentals=0),
        name="hand_down",
    )(filled, taken, solved)


def on_device(trailing, inverse_rows, rhs_tail, coupling, rhs_head, child_rows, owner):
    x = lax.axis_index("x")
    y = lax.axis_index("y")
    core = lax.axis_index("core")
    z = lax.axis_index("z")
    idx = jnp.stack([x, y, core, z]).astype(jnp.int32)
    rows, window = trailing.shape
    width = inverse_rows.shape[1]
    columns = rhs_tail.shape[1]
    part = columns // NY
    pair = 2 * width

    gathered = lax.all_gather(coupling, "z", axis=0, tiled=False)

    t_diag = lax.dynamic_slice(trailing, (0, pair * x + width), (rows, width))
    factors = jnp.concatenate([inverse_rows, t_diag], axis=1)
    right = rhs_tail.reshape(rows, NY, part).transpose(1, 0, 2)
    packed = jnp.concatenate([jnp.broadcast_to(factors, (NY,) + factors.shape), right], axis=2)
    packed = lax.all_to_all(packed, "y", split_axis=0, concat_axis=0, tiled=True)
    packed_other = both_cores(packed)
    r_own = packed[:, :, pair:]
    r_other = packed_other[:, :, pair:]

    chunks = {}
    after = packed
    for q in range(NX - 1, 0, -1):
        piece, _ = lax.optimization_barrier((trailing[:, q * pair : (q + 1) * pair], after))
        chunks[q] = exchange_y(piece)
        after = chunks[q][:2]

    halves = [None] * NX
    for p in range(NX - 1, -1, -1):
        mine = solve(p, idx, packed, packed_other, r_own, r_other, width)
        got = [lax.ppermute(mine, "x", [(p, (p + s) % NX)]) for s in (2, 3, 1)]
        halves[p] = jnp.where(x == p, mine, got[0] + got[1] + got[2])
        if p > 0:
            other = both_cores(halves[p])
            r_own = update(p, idx, halves[p], other, r_own, trailing, chunks[p])
            r_other = both_cores(r_own)
        if p == 2:
            first, _ = lax.optimization_barrier((halves[2:], r_own))
            first = jnp.stack(first)
            first_pieces = exchange_y(first, axis=1)
        if p == 1:
            second, _ = lax.optimization_barrier((halves[1][None], r_own))
            second_pieces = exchange_y(second, axis=1)
    first_pieces, second_pieces, last = lax.optimization_barrier((first_pieces, second_pieces, halves[0][None]))
    last_pieces = neighbours_y(last)
    first = join(idx, first, first_pieces)
    solved, top, low = assemble(idx, 2, first, both_cores(first), ())
    second = join(idx, second, second_pieces)
    solved, top2, low2 = assemble(idx, 1, second, both_cores(second), (solved,))
    top, last_pieces = lax.optimization_barrier((top, last_pieces))
    last_pieces = pass_on_y(*last_pieces, 1)
    remaining = product(rhs_head, gathered, top, low, 2)
    remaining = product(remaining, gathered, top2, low2, 1)
    last_pieces, remaining = lax.optimization_barrier((last_pieces, remaining))
    last = join(idx, last, last_pieces)
    solved, top, low = assemble(idx, 0, last, both_cores(last), (solved,))
    remaining = product(remaining, gathered, top, low, 0)

    group = (x * NY + y) * NC + core
    owned = (owner == group).astype(jnp.int32)
    rank = jnp.cumsum(owned) - owned
    slot_ids = jnp.arange(SLOTS, dtype=jnp.int32)
    picked = (owned[None, :] == 1) & (rank[None, :] == slot_ids[:, None])
    rows_taken = jnp.sum(jnp.where(picked[:, :, None], child_rows[None, :, :], 0), axis=1)
    filled = jnp.any(picked, axis=1)
    handed = hand(filled.astype(jnp.int32), rows_taken, solved)
    return (remaining, solved, handed)


def solution(mesh):
    grid = Mesh(mesh.devices.reshape(NX, NY, NC, -1), ROW + ("z",))
    return jax.shard_map(
        on_device,
        mesh=grid,
        in_specs=(
            P(ROW, None),
            P(ROW, None),
            P(ROW, "z"),
            P(ROW, "z"),
            P(ROW, "z"),
            P(),
            P(),
        ),
        out_specs=(P(ROW, "z"), P(None, "z"), P(ROW, None, "z")),
        check_vma=False,
    )
```

profile of v0, /device:TPU:1, one launch (start us, length us, event | category | flops | bytes accessed | tf_op | source)
XLA Modules:
  0.0 222.5 jit_solution(10589328934912215201)
XLA Ops:
  9.9 33.2 %all_to_all.5.fac_own = f32[4,128,1152]{2,1,0:T(8,128)S(1)} all-to-all(f32[4,128,1152]{2,1,0:T(8,128)S(1)} %pad_maximum_fusion), channel_id=1, replica_groups=mesh['x'=4,'y'=4,'core'=2,'z'=4] {'y'}, dimensions={0} | all-to-all | bytes 4718592 | tf_op jit(solution)/shard_map/all_to_all | solution.py:317
  43.1 1.9 collective-permute-start
  47.1 2.1 collective-permute-done.fac_other
  50.8 1.4 collective-permute-start.1
  52.2 1.4 collective-permute-start.2
  53.6 1.3 collective-permute-start.3
  54.9 6.3 %collective-permute-done.6.far = f32[128,1024]{1,0:T(8,128)S(1)} collective-permute-done((f32[128,1024]{1,0:T(8,128)}, f32[128,1024]{1,0:T(8,128)S(1)}, u32[]{:S(2)}, u32[]{:S(2)}) %collective-permute-start.6) | collective-permute-done | bytes 524320 | tf_op jit(solution)/shard_map/ppermute | solution.py:60
  63.4 4.9 %collective-permute-done.3 = f32[512,128]{1,0:T(8,128)} collective-permute-done((f32[512,128]{1,0:T(8,128)S(1)}, f32[512,128]{1,0:T(8,128)}, u32[]{:S(2)}, u32[]{:S(2)}) %collective-permute-start.3) | collective-permute-done | bytes 262176 | tf_op jit(solution)/shard_map/ppermute | solution.py:332
  72.7 2.9 %update_rows.3.r_own = f32[4,128,128]{2,1,0:T(8,128)S(1)} custom-call(s32[4]{0:T(128)S(1)} %pad_add_fusion.idx, f32[512,128]{1,0:T(8,128)S(1)} %add_select_fusion.2.mine, f32[512,128]{1,0:T(8,128)S(1)} %collective-permute-done.4.other, f32[4,128,128]{2,1,0:T(8,128)S(1)} %slice.68.r_own, f32[128,4096]{1,0:T(8,128)S(1)} %copy-done.2, ...), custom_call_target="tpu_custom_call" | custom-call | flops 1000 | bytes 1000 | tf_op jit(solution)/shard_map/update_rows/pallas_call | solution.py:155
  78.2 1.3 collective-permute-start.10
  79.5 1.4 collective-permute-start.11
  80.9 1.3 collective-permute-start.12
  82.2 3.3 %collective-permute-done.15.far = f32[128,1024]{1,0:T(8,128)} collective-permute-done((f32[128,1024]{1,0:T(8,128)}, f32[128,1024]{1,0:T(8,128)}, u32[]{:S(2)}, u32[]{:S(2)}) %collective-permute-start.15) | collective-permute-done | bytes 524320 | tf_op jit(solution)/shard_map/ppermute | solution.py:60
  88.5 3.4 %collective-permute-done.10 = f32[512,128]{1,0:T(8,128)S(1)} collective-permute-done((f32[512,128]{1,0:T(8,128)S(1)}, f32[512,128]{1,0:T(8,128)S(1)}, u32[]{:S(2)}, u32[]{:S(2)}) %collective-permute-start.10) | collective-permute-done | bytes 262176 | tf_op jit(solution)/shard_map/ppermute | solution.py:332
  93.8 1.4 collective-permute-start.13
  95.3 1.3 collective-permute-start.28
  97.7 3.3 %update_rows.4.r_own = f32[4,128,128]{2,1,0:T(8,128)S(1)} custom-call(s32[4]{0:T(128)S(1)} %pad_add_fusion.idx, f32[512,128]{1,0:T(8,128)S(1)} %add_select_fusion.1.mine, f32[512,128]{1,0:T(8,128)S(1)} %collective-permute-done.13.other, f32[4,128,128]{2,1,0:T(8,128)S(1)} %update_rows.3.r_own, f32[128,4096]{1,0:T(8,128)S(1)} %copy-done.3, ...), custom_call_target="tpu_custom_call" | custom-call | flops 1000 | bytes 1000 | tf_op jit(solution)/shard_map/update_rows/pallas_call | solution.py:155
  103.5 1.4 collective-permute-start.23
  104.9 1.3 collective-permute-start.24
  106.2 1.4 collective-permute-start.25
  107.5 2.8 %collective-permute-done.28.far = f32[128,1024]{1,0:T(8,128)} collective-permute-done((f32[128,1024]{1,0:T(8,128)}, f32[128,1024]{1,0:T(8,128)}, u32[]{:S(2)}, u32[]{:S(2)}) %collective-permute-start.28) | collective-permute-done | bytes 524320 | tf_op jit(solution)/shard_map/ppermute | solution.py:60
  112.3 1.8 collective-permute-start.30
  114.2 5.9 %collective-permute-done.24 = f32[512,128]{1,0:T(8,128)} collective-permute-done((f32[512,128]{1,0:T(8,128)S(1)}, f32[512,128]{1,0:T(8,128)}, u32[]{:S(2)}, u32[]{:S(2)}) %collective-permute-start.24) | collective-permute-done | bytes 262176 | tf_op jit(solution)/shard_map/ppermute | solution.py:332
  121.2 1.3 collective-permute-start.26
  123.8 3.1 %update_rows.5.r_own = f32[4,128,128]{2,1,0:T(8,128)S(1)} custom-call(s32[4]{0:T(128)S(1)} %pad_add_fusion.idx, f32[512,128]{1,0:T(8,128)S(1)} %add_select_fusion.mine, f32[512,128]{1,0:T(8,128)S(1)} %collective-permute-done.26.other, f32[4,128,128]{2,1,0:T(8,128)S(1)} %update_rows.4.r_own, f32[128,4096]{1,0:T(8,128)S(1)} %copy-done.4, ...), custom_call_target="tpu_custom_call" | custom-call | flops 1000 | bytes 1000 | tf_op jit(solution)/shard_map/update_rows/pallas_call | solution.py:155
  130.0 3.9 %solve_pair.7 = f32[512,128]{1,0:T(8,128)S(1)} custom-call(s32[4]{0:T(128)S(1)} %pad_add_fusion.idx, f32[4,128,1152]{2,1,0:T(8,128)S(1)} %all_to_all.5.fac_own, f32[4,128,1152]{2,1,0:T(8,128)} %collective-permute-done.fac_other, f32[4,128,128]{2,1,0:T(8,128)S(1)} %update_rows.5.r_own, f32[4,128,128]{2,1,0:T(8,128)S(1)} %collective-permute-done.35.r_other), custom_call_target="tpu_custom_call" | custom-call | flops 1000 | bytes 1000 | tf_op jit(solution)/shard_map/solve_pair/pallas_call | solution.py:109
  134.0 1.4 collective-permute-start.36
  135.4 2.1 collective-permute-done.19.far
  137.5 1.6 collective-permute-start.37
  139.1 1.3 collective-permute-start.38
  146.9 1.8 collective-permute-start.34
  150.3 2.6 %collective-permute-done.33.top = f32[1,256,128]{2,1,0:T(8,128)S(1)} collective-permute-done((f32[1,256,128]{2,1,0:T(8,128)S(1)}, f32[1,256,128]{2,1,0:T(8,128)S(1)}, u32[]{:S(2)}, u32[]{:S(2)}) %collective-permute-start.33) | collective-permute-done | bytes 131104 | tf_op jit(solution)/shard_map/ppermute | solution.py:65
  154.5 3.3 %collective-permute-start.39 = (f32[2,512,512]{2,1,0:T(8,128)S(1)}, f32[2,512,512]{2,1,0:T(8,128)S(1)}, u32[]{:S(2)}, u32[]{:S(2)}) collective-permute-start(f32[2,512,512]{2,1,0:T(8,128)S(1)} %join_columns.3.own), channel_id=1, source_target_pairs={{0,4},{4,0},{1,5},{5,1},{2,6},{6,2},{3,7},{7,3},{8,12},{12,8},{9,1... | collective-permute-start | bytes 6291464 | tf_op jit(solution)/shard_map/ppermute | solution.py:53
  157.9 1.7 join_columns.4.own
  161.7 3.0 %assemble_pairs.3 = (f32[4096,512]{1,0:T(8,128)}, bf16[2,1024,512]{2,1,0:T(8,128)(2,1)S(1)}, bf16[2,1024,512]{2,1,0:T(8,128)(2,1)S(1)}) custom-call(s32[4]{0:T(128)S(1)} %pad_add_fusion.idx, f32[2,512,512]{2,1,0:T(8,128)S(1)} %join_columns.3.own, f32[2,512,512]{2,1,0:T(8,128)S(1)} %collective-permute-done.39.other), custom_call_target="tpu_custom_call" | custom-call | bytes 12582912 | tf_op jit(solution)/shard_map/assemble_pairs/pallas_call | solution.py:222
  164.7 1.3 copy-done.6
  166.0 1.3 copy-done.8
  170.7 2.2 assemble_pairs.4
  173.9 1.6 copy-done.7
  175.5 1.6 copy-done.9
  177.1 9.0 %product.3.start = f32[1024,512]{1,0:T(8,128)S(1)} custom-call(f32[1024,512]{1,0:T(8,128)S(1)} %copy-done.5, f32[4,1024,1024]{2,1,0:T(8,128)} %bitcast.19, bf16[2,1024,512]{2,1,0:T(8,128)(2,1)S(1)} %copy-done.7, bf16[2,1024,512]{2,1,0:T(8,128)(2,1)S(1)} %copy-done.9), custom_call_target="tpu_custom_call" | custom-call | flops 6442450944 | bytes 16777216 | tf_op jit(solution)/shard_map/product/pallas_call | solution.py:250
  186.2 5.5 %product.4.start = f32[1024,512]{1,0:T(8,128)S(1)} custom-call(f32[1024,512]{1,0:T(8,128)S(1)} %product.3.start, f32[4,1024,1024]{2,1,0:T(8,128)} %bitcast.20, bf16[1,1024,512]{2,1,0:T(8,128)(2,1)S(1)} %get-tuple-element.56.b_top, bf16[1,1024,512]{2,1,0:T(8,128)(2,1)S(1)} %copy-done.17), custom_call_target="tpu_custom_call" | custom-call | flops 3221225472 | bytes 8388608 | tf_op jit(solution)/shard_map/product/pallas_call | solution.py:250
  191.8 1.6 join_columns.5.own
  193.4 2.0 collective-permute-start.45
  197.9 3.0 %assemble_pairs.5 = (f32[4096,512]{1,0:T(8,128)}, bf16[1,1024,512]{2,1,0:T(8,128)(2,1)S(1)}, bf16[1,1024,512]{2,1,0:T(8,128)(2,1)S(1)}) custom-call(s32[4]{0:T(128)S(1)} %pad_add_fusion.idx, f32[1,512,512]{2,1,0:T(8,128)S(1)} %join_columns.5.own, f32[1,512,512]{2,1,0:T(8,128)} %collective-permute-done.45.other, ...), custom_call_target="tpu_custom_call", output_to_operand_aliasing={{0}: (3, {})} | custom-call | bytes 6291456 | tf_op jit(solution)/shard_map/assemble_pairs/pallas_call | solution.py:222
  200.9 3.4 %copy-done = f32[4096,512]{1,0:T(8,128)S(1)} copy-done((f32[4096,512]{1,0:T(8,128)S(1)}, f32[4096,512]{1,0:T(8,128)}, u32[]{:S(2)}) %copy-start) | copy-done | bytes 8388632
  204.3 5.0 %hand_down.1 = f32[4,256,512]{2,1,0:T(8,128)} custom-call(s32[4]{0:T(128)S(1)} %convert_element_type.7.filled, s32[4,256]{1,0:T(4,128)S(1)} %select_reduce_fusion.taken, f32[4096,512]{1,0:T(8,128)S(1)} %copy-done), custom_call_target="tpu_custom_call" | custom-call | bytes 10485760 | tf_op jit(solution)/shard_map/hand_down/pallas_call | solution.py:287
  209.2 6.5 %product.5 = f32[1024,512]{1,0:T(8,128)} custom-call(f32[1024,512]{1,0:T(8,128)S(1)} %product.4.start, f32[4,1024,1024]{2,1,0:T(8,128)} %bitcast.21, bf16[1,1024,512]{2,1,0:T(8,128)(2,1)S(1)} %get-tuple-element.64.b_top, bf16[1,1024,512]{2,1,0:T(8,128)(2,1)S(1)} %get-tuple-element.65.b_low), custom_call_target="tpu_custom_call" | custom-call | flops 3221225472 | bytes 8388608 | tf_op jit(solution)/shard_map/product/pallas_call | solution.py:250
  (156 shorter events, 50.2 us)
Async XLA Ops:
  7.2 166.8 %all-gather.3.cloned.1.call-start = ((), (), s32[]{:S(2)}) async-start(), calls=%async_computation.1 | async-start | bytes 20971520 | tf_op jit(solution)/shard_map/all_gather | solution.py:311
  9.9 35.1 %copy-start.1 = (f32[128,4096]{1,0:T(8,128)S(1)}, f32[128,4096]{1,0:T(8,128)}, u32[]{:S(2)}) copy-start(f32[128,4096]{1,0:T(8,128)} %trailing.5) | copy-start | bytes 6291460
  43.1 6.2 %collective-permute-start = (f32[4,128,1152]{2,1,0:T(8,128)S(1)}, f32[4,128,1152]{2,1,0:T(8,128)}, u32[]{:S(2)}, u32[]{:S(2)}) collective-permute-start(f32[4,128,1152]{2,1,0:T(8,128)S(1)} %all_to_all.5.fac_own), channel_id=1, source_target_pairs={{0,4},{4,0},{1,5},{5,1},{2,6},{6,2},{3,7},{7,3},{8,12},{12,8},{9,1... | collective-permute-start | bytes 7077896 | tf_op jit(solution)/shard_map/ppermute | solution.py:53
  46.1 15.1 %collective-permute-start.6 = (f32[128,1024]{1,0:T(8,128)}, f32[128,1024]{1,0:T(8,128)S(1)}, u32[]{:S(2)}, u32[]{:S(2)}) collective-permute-start(f32[128,1024]{1,0:T(8,128)} %get-tuple-element.35), channel_id=1, source_target_pairs={{0,24},{8,16},{16,8},{24,0},{1,25},{9,17},{17,9},{25,1},{2,26},{10... | collective-permute-start | bytes 1572872 | tf_op jit(solution)/shard_map/ppermute | solution.py:60
  47.0 14.3 %collective-permute-start.5 = (f32[128,1024]{1,0:T(8,128)}, f32[128,1024]{1,0:T(8,128)}, u32[]{:S(2)}, u32[]{:S(2)}) collective-permute-start(f32[128,1024]{1,0:T(8,128)} %get-tuple-element.35), channel_id=1, source_target_pairs={{0,8},{8,0},{16,24},{24,16},{1,9},{9,1},{17,25},{25,17},{2,10},{10... | collective-permute-start | bytes 1572872 | tf_op jit(solution)/shard_map/ppermute | solution.py:60
  50.8 12.6 %collective-permute-start.1 = (f32[512,128]{1,0:T(8,128)S(1)}, f32[512,128]{1,0:T(8,128)}, u32[]{:S(2)}, u32[]{:S(2)}) collective-permute-start(f32[512,128]{1,0:T(8,128)S(1)} %solve_pair.4), channel_id=1, source_target_pairs={{96,32},{97,33},{98,34},{99,35},{100,36},{101,37},{102,38},{103,39... | collective-permute-start | bytes 786440 | tf_op jit(solution)/shard_map/ppermute | solution.py:332
  52.2 11.2 %collective-permute-start.2 = (f32[512,128]{1,0:T(8,128)S(1)}, f32[512,128]{1,0:T(8,128)}, u32[]{:S(2)}, u32[]{:S(2)}) collective-permute-start(f32[512,128]{1,0:T(8,128)S(1)} %solve_pair.4), channel_id=1, source_target_pairs={{96,64},{97,65},{98,66},{99,67},{100,68},{101,69},{102,70},{103,71... | collective-permute-start | bytes 786440 | tf_op jit(solution)/shard_map/ppermute | solution.py:332
  53.6 14.8 %collective-permute-start.3 = (f32[512,128]{1,0:T(8,128)S(1)}, f32[512,128]{1,0:T(8,128)}, u32[]{:S(2)}, u32[]{:S(2)}) collective-permute-start(f32[512,128]{1,0:T(8,128)S(1)} %solve_pair.4), channel_id=1, source_target_pairs={{96,0},{97,1},{98,2},{99,3},{100,4},{101,5},{102,6},{103,7},{104,8... | collective-permute-start | bytes 786440 | tf_op jit(solution)/shard_map/ppermute | solution.py:332
  61.2 10.2 %collective-permute-start.7 = (f32[64,1024]{1,0:T(8,128)S(1)}, f32[64,1024]{1,0:T(8,128)S(1)}, u32[]{:S(2)}, u32[]{:S(2)}) collective-permute-start(f32[64,1024]{1,0:T(8,128)S(1)} %slice.70), channel_id=1, source_target_pairs={{0,8},{8,0},{16,24},{24,16},{1,9},{9,1},{17,25},{25,17},{2,10},{10... | collective-permute-start | bytes 786440 | tf_op jit(solution)/shard_map/ppermute | solution.py:65
  62.4 9.0 %collective-permute-start.8 = (f32[64,1024]{1,0:T(8,128)S(1)}, f32[64,1024]{1,0:T(8,128)S(1)}, u32[]{:S(2)}, u32[]{:S(2)}) collective-permute-start(f32[64,1024]{1,0:T(8,128)S(1)} %slice.71), channel_id=1, source_target_pairs={{0,24},{8,16},{16,8},{24,0},{1,25},{9,17},{17,9},{25,1},{2,26},{10... | collective-permute-start | bytes 786440 | tf_op jit(solution)/shard_map/ppermute | solution.py:66
  69.5 2.1 collective-permute-start.4
  70.5 15.0 %collective-permute-start.15 = (f32[128,1024]{1,0:T(8,128)}, f32[128,1024]{1,0:T(8,128)}, u32[]{:S(2)}, u32[]{:S(2)}) collective-permute-start(f32[128,1024]{1,0:T(8,128)} %get-tuple-element.36), channel_id=1, source_target_pairs={{0,24},{8,16},{16,8},{24,0},{1,25},{9,17},{17,9},{25,1},{2,26},{10... | collective-permute-start | bytes 1572872 | tf_op jit(solution)/shard_map/ppermute | solution.py:60
  71.4 15.2 %collective-permute-start.14 = (f32[128,1024]{1,0:T(8,128)}, f32[128,1024]{1,0:T(8,128)}, u32[]{:S(2)}, u32[]{:S(2)}) collective-permute-start(f32[128,1024]{1,0:T(8,128)} %get-tuple-element.36), channel_id=1, source_target_pairs={{0,8},{8,0},{16,24},{24,16},{1,9},{9,1},{17,25},{25,17},{2,10},{10... | collective-permute-start | bytes 1572872 | tf_op jit(solution)/shard_map/ppermute | solution.py:60
  75.6 2.0 collective-permute-start.9
  78.2 13.7 %collective-permute-start.10 = (f32[512,128]{1,0:T(8,128)S(1)}, f32[512,128]{1,0:T(8,128)S(1)}, u32[]{:S(2)}, u32[]{:S(2)}) collective-permute-start(f32[512,128]{1,0:T(8,128)S(1)} %solve_pair.5), channel_id=1, source_target_pairs={{64,0},{65,1},{66,2},{67,3},{68,4},{69,5},{70,6},{71,7},{72,8},{73... | collective-permute-start | bytes 786440 | tf_op jit(solution)/shard_map/ppermute | solution.py:332
  79.5 12.4 %collective-permute-start.11 = (f32[512,128]{1,0:T(8,128)S(1)}, f32[512,128]{1,0:T(8,128)}, u32[]{:S(2)}, u32[]{:S(2)}) collective-permute-start(f32[512,128]{1,0:T(8,128)S(1)} %solve_pair.5), channel_id=1, source_target_pairs={{64,32},{65,33},{66,34},{67,35},{68,36},{69,37},{70,38},{71,39},{7... | collective-permute-start | bytes 786440 | tf_op jit(solution)/shard_map/ppermute | solution.py:332
  80.9 11.8 %collective-permute-start.12 = (f32[512,128]{1,0:T(8,128)S(1)}, f32[512,128]{1,0:T(8,128)}, u32[]{:S(2)}, u32[]{:S(2)}) collective-permute-start(f32[512,128]{1,0:T(8,128)S(1)} %solve_pair.5), channel_id=1, source_target_pairs={{64,96},{65,97},{66,98},{67,99},{68,100},{69,101},{70,102},{71,103... | collective-permute-start | bytes 786440 | tf_op jit(solution)/shard_map/ppermute | solution.py:332
  86.5 11.2 %collective-permute-start.16 = (f32[64,1024]{1,0:T(8,128)S(1)}, f32[64,1024]{1,0:T(8,128)S(1)}, u32[]{:S(2)}, u32[]{:S(2)}) collective-permute-start(f32[64,1024]{1,0:T(8,128)S(1)} %slice.72), channel_id=1, source_target_pairs={{0,8},{8,0},{16,24},{24,16},{1,9},{9,1},{17,25},{25,17},{2,10},{10... | collective-permute-start | bytes 786440 | tf_op jit(solution)/shard_map/ppermute | solution.py:65
  87.5 10.1 %collective-permute-start.17 = (f32[64,1024]{1,0:T(8,128)S(1)}, f32[64,1024]{1,0:T(8,128)S(1)}, u32[]{:S(2)}, u32[]{:S(2)}) collective-permute-start(f32[64,1024]{1,0:T(8,128)S(1)} %slice.73), channel_id=1, source_target_pairs={{0,24},{8,16},{16,8},{24,0},{1,25},{9,17},{17,9},{25,1},{2,26},{10... | collective-permute-start | bytes 786440 | tf_op jit(solution)/shard_map/ppermute | solution.py:66
  93.8 3.9 %collective-permute-start.13 = (f32[512,128]{1,0:T(8,128)S(1)}, f32[512,128]{1,0:T(8,128)S(1)}, u32[]{:S(2)}, u32[]{:S(2)}) collective-permute-start(f32[512,128]{1,0:T(8,128)S(1)} %add_select_fusion.1.mine), channel_id=1, source_target_pairs={{0,4},{4,0},{1,5},{5,1},{2,6},{6,2},{3,7},{7,3},{8,12},{12,8},{9,1... | collective-permute-start | bytes 786440 | tf_op jit(solution)/shard_map/ppermute | solution.py:53
  95.3 15.0 %collective-permute-start.28 = (f32[128,1024]{1,0:T(8,128)}, f32[128,1024]{1,0:T(8,128)}, u32[]{:S(2)}, u32[]{:S(2)}) collective-permute-start(f32[128,1024]{1,0:T(8,128)} %get-tuple-element.39), channel_id=1, source_target_pairs={{0,24},{8,16},{16,8},{24,0},{1,25},{9,17},{17,9},{25,1},{2,26},{10... | collective-permute-start | bytes 1572872 | tf_op jit(solution)/shard_map/ppermute | solution.py:60
  96.6 14.8 %collective-permute-start.27 = (f32[128,1024]{1,0:T(8,128)}, f32[128,1024]{1,0:T(8,128)}, u32[]{:S(2)}, u32[]{:S(2)}) collective-permute-start(f32[128,1024]{1,0:T(8,128)} %get-tuple-element.39), channel_id=1, source_target_pairs={{0,8},{8,0},{16,24},{24,16},{1,9},{9,1},{17,25},{25,17},{2,10},{10... | collective-permute-start | bytes 1572872 | tf_op jit(solution)/shard_map/ppermute | solution.py:60
  101.0 1.9 collective-permute-start.22
  103.5 10.7 %collective-permute-start.23 = (f32[512,128]{1,0:T(8,128)S(1)}, f32[512,128]{1,0:T(8,128)}, u32[]{:S(2)}, u32[]{:S(2)}) collective-permute-start(f32[512,128]{1,0:T(8,128)S(1)} %solve_pair.6), channel_id=1, source_target_pairs={{32,96},{33,97},{34,98},{35,99},{36,100},{37,101},{38,102},{39,103... | collective-permute-start | bytes 786440 | tf_op jit(solution)/shard_map/ppermute | solution.py:332
  104.9 15.2 %collective-permute-start.24 = (f32[512,128]{1,0:T(8,128)S(1)}, f32[512,128]{1,0:T(8,128)}, u32[]{:S(2)}, u32[]{:S(2)}) collective-permute-start(f32[512,128]{1,0:T(8,128)S(1)} %solve_pair.6), channel_id=1, source_target_pairs={{32,0},{33,1},{34,2},{35,3},{36,4},{37,5},{38,6},{39,7},{40,8},{41... | collective-permute-start | bytes 786440 | tf_op jit(solution)/shard_map/ppermute | solution.py:332
  106.2 13.9 %collective-permute-start.25 = (f32[512,128]{1,0:T(8,128)S(1)}, f32[512,128]{1,0:T(8,128)}, u32[]{:S(2)}, u32[]{:S(2)}) collective-permute-start(f32[512,128]{1,0:T(8,128)S(1)} %solve_pair.6), channel_id=1, source_target_pairs={{32,64},{33,65},{34,66},{35,67},{36,68},{37,69},{38,70},{39,71},{4... | collective-permute-start | bytes 786440 | tf_op jit(solution)/shard_map/ppermute | solution.py:332
  111.3 12.5 %collective-permute-start.29 = (f32[64,1024]{1,0:T(8,128)S(1)}, f32[64,1024]{1,0:T(8,128)S(1)}, u32[]{:S(2)}, u32[]{:S(2)}) collective-permute-start(f32[64,1024]{1,0:T(8,128)S(1)} %slice.76), channel_id=1, source_target_pairs={{0,8},{8,0},{16,24},{24,16},{1,9},{9,1},{17,25},{25,17},{2,10},{10... | collective-permute-start | bytes 786440 | tf_op jit(solution)/shard_map/ppermute | solution.py:65
  112.3 11.5 %collective-permute-start.30 = (f32[64,1024]{1,0:T(8,128)S(1)}, f32[64,1024]{1,0:T(8,128)S(1)}, u32[]{:S(2)}, u32[]{:S(2)}) collective-permute-start(f32[64,1024]{1,0:T(8,128)S(1)} %slice.77), channel_id=1, source_target_pairs={{0,24},{8,16},{16,8},{24,0},{1,25},{9,17},{17,9},{25,1},{2,26},{10... | collective-permute-start | bytes 786440 | tf_op jit(solution)/shard_map/ppermute | solution.py:66
  121.2 2.6 %collective-permute-start.26 = (f32[512,128]{1,0:T(8,128)S(1)}, f32[512,128]{1,0:T(8,128)S(1)}, u32[]{:S(2)}, u32[]{:S(2)}) collective-permute-start(f32[512,128]{1,0:T(8,128)S(1)} %add_select_fusion.mine), channel_id=1, source_target_pairs={{0,4},{4,0},{1,5},{5,1},{2,6},{6,2},{3,7},{7,3},{8,12},{12,8},{9,1... | collective-permute-start | bytes 786440 | tf_op jit(solution)/shard_map/ppermute | solution.py:53
  122.6 14.9 %collective-permute-start.19 = (f32[2,512,128]{2,1,0:T(8,128)S(1)}, f32[2,512,128]{2,1,0:T(8,128)S(1)}, u32[]{:S(2)}, u32[]{:S(2)}) collective-permute-start(f32[2,512,128]{2,1,0:T(8,128)S(1)} %pad_maximum_fusion.2.own), channel_id=1, source_target_pairs={{0,24},{8,16},{16,8},{24,0},{1,25},{9,17},{17,9},{25,1},{2,26},{10... | collective-permute-start | bytes 1572872 | tf_op jit(solution)/shard_map/ppermute | solution.py:60
  123.5 15.5 %collective-permute-start.18 = (f32[2,512,128]{2,1,0:T(8,128)S(1)}, f32[2,512,128]{2,1,0:T(8,128)S(1)}, u32[]{:S(2)}, u32[]{:S(2)}) collective-permute-start(f32[2,512,128]{2,1,0:T(8,128)S(1)} %pad_maximum_fusion.2.own), channel_id=1, source_target_pairs={{0,8},{8,0},{16,24},{24,16},{1,9},{9,1},{17,25},{25,17},{2,10},{10... | collective-permute-start | bytes 1572872 | tf_op jit(solution)/shard_map/ppermute | solution.py:60
  127.0 3.1 %collective-permute-start.35 = (f32[4,128,128]{2,1,0:T(8,128)S(1)}, f32[4,128,128]{2,1,0:T(8,128)S(1)}, u32[]{:S(2)}, u32[]{:S(2)}) collective-permute-start(f32[4,128,128]{2,1,0:T(8,128)S(1)} %update_rows.5.r_own), channel_id=1, source_target_pairs={{0,4},{4,0},{1,5},{5,1},{2,6},{6,2},{3,7},{7,3},{8,12},{12,8},{9,1... | collective-permute-start | bytes 786440 | tf_op jit(solution)/shard_map/ppermute | solution.py:53
  127.6 15.5 %collective-permute-start.32 = (f32[1,512,128]{2,1,0:T(8,128)S(1)}, f32[1,512,128]{2,1,0:T(8,128)}, u32[]{:S(2)}, u32[]{:S(2)}) collective-permute-start(f32[1,512,128]{2,1,0:T(8,128)S(1)} %bitcast.14), channel_id=1, source_target_pairs={{0,24},{8,16},{16,8},{24,0},{1,25},{9,17},{17,9},{25,1},{2,26},{10... | collective-permute-start | bytes 786440 | tf_op jit(solution)/shard_map/ppermute | solution.py:60
  128.9 14.2 %collective-permute-start.31 = (f32[1,512,128]{2,1,0:T(8,128)S(1)}, f32[1,512,128]{2,1,0:T(8,128)}, u32[]{:S(2)}, u32[]{:S(2)}) collective-permute-start(f32[1,512,128]{2,1,0:T(8,128)S(1)} %bitcast.15), channel_id=1, source_target_pairs={{0,8},{8,0},{16,24},{24,16},{1,9},{9,1},{17,25},{25,17},{2,10},{10... | collective-permute-start | bytes 786440 | tf_op jit(solution)/shard_map/ppermute | solution.py:60
  134.0 12.2 %collective-permute-start.36 = (f32[512,128]{1,0:T(8,128)S(1)}, f32[512,128]{1,0:T(8,128)S(1)}, u32[]{:S(2)}, u32[]{:S(2)}) collective-permute-start(f32[512,128]{1,0:T(8,128)S(1)} %solve_pair.7), channel_id=1, source_target_pairs={{0,64},{1,65},{2,66},{3,67},{4,68},{5,69},{6,70},{7,71},{8,72},{9,... | collective-permute-start | bytes 786440 | tf_op jit(solution)/shard_map/ppermute | solution.py:332
  137.5 9.4 %collective-permute-start.37 = (f32[512,128]{1,0:T(8,128)S(1)}, f32[512,128]{1,0:T(8,128)S(1)}, u32[]{:S(2)}, u32[]{:S(2)}) collective-permute-start(f32[512,128]{1,0:T(8,128)S(1)} %solve_pair.7), channel_id=1, source_target_pairs={{0,96},{1,97},{2,98},{3,99},{4,100},{5,101},{6,102},{7,103},{8,104... | collective-permute-start | bytes 786440 | tf_op jit(solution)/shard_map/ppermute | solution.py:332
  139.1 9.6 %collective-permute-start.38 = (f32[512,128]{1,0:T(8,128)S(1)}, f32[512,128]{1,0:T(8,128)S(1)}, u32[]{:S(2)}, u32[]{:S(2)}) collective-permute-start(f32[512,128]{1,0:T(8,128)S(1)} %solve_pair.7), channel_id=1, source_target_pairs={{0,32},{1,33},{2,34},{3,35},{4,36},{5,37},{6,38},{7,39},{8,40},{9,... | collective-permute-start | bytes 786440 | tf_op jit(solution)/shard_map/ppermute | solution.py:332
  143.1 6.9 %collective-permute-start.20 = (f32[2,256,128]{2,1,0:T(8,128)}, f32[2,256,128]{2,1,0:T(8,128)S(1)}, u32[]{:S(2)}, u32[]{:S(2)}) collective-permute-start(f32[2,256,128]{2,1,0:T(8,128)} %slice.74), channel_id=1, source_target_pairs={{0,8},{8,0},{16,24},{24,16},{1,9},{9,1},{17,25},{25,17},{2,10},{10... | collective-permute-start | bytes 786440 | tf_op jit(solution)/shard_map/ppermute | solution.py:65
  143.1 7.1 %collective-permute-start.21 = (f32[2,256,128]{2,1,0:T(8,128)}, f32[2,256,128]{2,1,0:T(8,128)S(1)}, u32[]{:S(2)}, u32[]{:S(2)}) collective-permute-start(f32[2,256,128]{2,1,0:T(8,128)} %slice.75), channel_id=1, source_target_pairs={{0,24},{8,16},{16,8},{24,0},{1,25},{9,17},{17,9},{25,1},{2,26},{10... | collective-permute-start | bytes 786440 | tf_op jit(solution)/shard_map/ppermute | solution.py:66
  146.2 6.7 %collective-permute-start.33 = (f32[1,256,128]{2,1,0:T(8,128)S(1)}, f32[1,256,128]{2,1,0:T(8,128)S(1)}, u32[]{:S(2)}, u32[]{:S(2)}) collective-permute-start(f32[1,256,128]{2,1,0:T(8,128)S(1)} %slice.78), channel_id=1, source_target_pairs={{0,8},{8,0},{16,24},{24,16},{1,9},{9,1},{17,25},{25,17},{2,10},{10... | collective-permute-start | bytes 393224 | tf_op jit(solution)/shard_map/ppermute | solution.py:65
  146.9 6.8 %collective-permute-start.34 = (f32[1,256,128]{2,1,0:T(8,128)S(1)}, f32[1,256,128]{2,1,0:T(8,128)S(1)}, u32[]{:S(2)}, u32[]{:S(2)}) collective-permute-start(f32[1,256,128]{2,1,0:T(8,128)S(1)} %slice.79), channel_id=1, source_target_pairs={{0,24},{8,16},{16,8},{24,0},{1,25},{9,17},{17,9},{25,1},{2,26},{10... | collective-permute-start | bytes 393224 | tf_op jit(solution)/shard_map/ppermute | solution.py:66
  154.5 7.1 %collective-permute-start.39 = (f32[2,512,512]{2,1,0:T(8,128)S(1)}, f32[2,512,512]{2,1,0:T(8,128)S(1)}, u32[]{:S(2)}, u32[]{:S(2)}) collective-permute-start(f32[2,512,512]{2,1,0:T(8,128)S(1)} %join_columns.3.own), channel_id=1, source_target_pairs={{0,4},{4,0},{1,5},{5,1},{2,6},{6,2},{3,7},{7,3},{8,12},{12,8},{9,1... | collective-permute-start | bytes 6291464 | tf_op jit(solution)/shard_map/ppermute | solution.py:53
  159.6 11.2 %collective-permute-start.44 = (f32[1,512,512]{2,1,0:T(8,128)S(1)}, f32[1,512,512]{2,1,0:T(8,128)S(1)}, u32[]{:S(2)}, u32[]{:S(2)}) collective-permute-start(f32[1,512,512]{2,1,0:T(8,128)S(1)} %join_columns.4.own), channel_id=1, source_target_pairs={{0,4},{4,0},{1,5},{5,1},{2,6},{6,2},{3,7},{7,3},{8,12},{12,8},{9,1... | collective-permute-start | bytes 3145736 | tf_op jit(solution)/shard_map/ppermute | solution.py:53
  159.7 7.7 %collective-permute-start.40 = (f32[1,512,128]{2,1,0:T(8,128)S(1)}, f32[1,512,128]{2,1,0:T(8,128)S(1)}, u32[]{:S(2)}, u32[]{:S(2)}) collective-permute-start(f32[1,512,128]{2,1,0:T(8,128)S(1)} %select_bitcast_fusion.own), channel_id=1, source_target_pairs={{0,8},{8,0},{16,24},{24,16},{1,9},{9,1},{17,25},{25,17},{2,10},{10... | collective-permute-start | bytes 786440 | tf_op jit(solution)/shard_map/ppermute | solution.py:60
  159.8 8.9 %collective-permute-start.41 = (f32[1,512,128]{2,1,0:T(8,128)S(1)}, f32[1,512,128]{2,1,0:T(8,128)S(1)}, u32[]{:S(2)}, u32[]{:S(2)}) collective-permute-start(f32[1,512,128]{2,1,0:T(8,128)S(1)} %select_bitcast_fusion.own), channel_id=1, source_target_pairs={{0,24},{8,16},{16,8},{24,0},{1,25},{9,17},{17,9},{25,1},{2,26},{10... | collective-permute-start | bytes 786440 | tf_op jit(solution)/shard_map/ppermute | solution.py:60
  169.3 22.5 %collective-permute-start.42 = (f32[1,256,128]{2,1,0:T(8,128)}, f32[1,256,128]{2,1,0:T(8,128)S(1)}, u32[]{:S(2)}, u32[]{:S(2)}) collective-permute-start(f32[1,256,128]{2,1,0:T(8,128)} %slice.66), channel_id=1, source_target_pairs={{0,8},{8,0},{16,24},{24,16},{1,9},{9,1},{17,25},{25,17},{2,10},{10... | collective-permute-start | bytes 393224 | tf_op jit(solution)/shard_map/ppermute | solution.py:65
  170.0 21.8 %collective-permute-start.43 = (f32[1,256,128]{2,1,0:T(8,128)}, f32[1,256,128]{2,1,0:T(8,128)}, u32[]{:S(2)}, u32[]{:S(2)}) collective-permute-start(f32[1,256,128]{2,1,0:T(8,128)} %slice.67), channel_id=1, source_target_pairs={{0,24},{8,16},{16,8},{24,0},{1,25},{9,17},{17,9},{25,1},{2,26},{10... | collective-permute-start | bytes 393224 | tf_op jit(solution)/shard_map/ppermute | solution.py:66
  193.4 4.4 %collective-permute-start.45 = (f32[1,512,512]{2,1,0:T(8,128)S(1)}, f32[1,512,512]{2,1,0:T(8,128)}, u32[]{:S(2)}, u32[]{:S(2)}) collective-permute-start(f32[1,512,512]{2,1,0:T(8,128)S(1)} %join_columns.5.own), channel_id=1, source_target_pairs={{0,4},{4,0},{1,5},{5,1},{2,6},{6,2},{3,7},{7,3},{8,12},{12,8},{9,1... | collective-permute-start | bytes 3145736 | tf_op jit(solution)/shard_map/ppermute | solution.py:53
  (27 other events, 174.0 us)
Sparse Core Ops, SparseCore 0:
  9.7 157.3 all-gather.2
where the time goes:
time: 225 us; the launch traced here: 223 us
  Pallas kernels  53.5 us (24%)
  starting transfers between devices  47.2 us (21%)
  waiting for transfers between devices  42.3 us (19%)
  blocking collectives  33.2 us (15%)
  local copies, waits for them, and re-layouts  25.6 us (11%)
  between operations  14.6 us (6%)
  other arithmetic  6.16 us (3%)
    all_to_all x1, blocking collectives, on_device(): lax.all_to_all(packed, 'y', split_axis=0, concat_axis=0, tiled=True)  33.2 us
    pallas_call x3, Pallas kernels, product(): pl.pallas_call(product_kernel, grid=(rows // tile, count), out_shape=jax....  21.1 us
    ppermute x12, waiting for transfers between devices, neighbours_y(): return (lax.ppermute(piece, 'y', ONE), lax.ppermute(piece, 'y', THREE))  17 us
    ppermute x12, starting transfers between devices, on_device(): got = [lax.ppermute(mine, 'x', [(p, (p + s) % NX)]) for s in (2, 3, 1)]  16.3 us
    ppermute x12, waiting for transfers between devices, on_device(): got = [lax.ppermute(mine, 'x', [(p, (p + s) % NX)]) for s in (2, 3, 1)]  14.3 us
    ppermute x10, starting transfers between devices, both_cores(): return lax.ppermute(own, 'core', SWAP)  13.2 us
    unnamed x57, local copies, waits for them, and re-layouts  12.4 us
    pallas_call x3, Pallas kernels, update(): pl.pallas_call(functools.partial(update_kernel, p), out_shape=jax.ShapeDt...  9.37 us
  transfers between devices with their start and end apart: 47, of which 19 were waited for; matrix products, arithmetic and copies ran while one was open for 9% of the time, Pallas kernels for 17%

commit v1 on v0

--- a/solution.py
+++ b/solution.py
@@ -164,136 +164,157 @@
     )(idx, mine, other, r_own, trailing, *pieces)
 
 
-def join_kernel(idx, own, near, far, top, bottom, out, sems):
+def join_kernel(groups, idx, *refs):
     y = idx[1]
-    height, part = own.shape[1:]
-    half = height // 2
-
-    def columns(s):
-        return pl.ds(pl.multiple_of((y ^ s) * part, part), part)
-
-    moves = (
-        (own, out.at[:, :, columns(0)]),
-        (near, out.at[:, :, columns(1)]),
-        (far, out.at[:, :, columns(3)]),
-        (top, out.at[:, pl.ds(0, half), columns(2)]),
-        (bottom, out.at[:, pl.ds(half, half), columns(2)]),
-    )
-    copies = [pltpu.make_async_copy(src, dst, sems.at[n]) for n, (src, dst) in enumerate(moves)]
+    out, sems = refs[-2:]
+    copies = []
+    base = 0
+    refs = list(refs[:-2])
+    for count in groups:
+        pieces, refs = refs[:count], refs[count:]
+        n, height, part = pieces[0].shape
+        for m, (piece, s) in enumerate(zip(pieces, (0, 1, 3, 2, 2))):
+            rows = pl.ds(height // 2 if m == 4 else 0, piece.shape[1])
+            columns = pl.ds(pl.multiple_of((y ^ s) * part, part), part)
+            dst = out.at[pl.ds(base, n), rows, columns]
+            copies.append(pltpu.make_async_copy(piece, dst, sems.at[len(copies)]))
+        base += n
     for cp in copies:
         cp.start()
     for cp in copies:
         cp.wait()
 
 
-def join(idx, own, pieces):
-    n, height, part = own.shape
+def join(idx, *groups):
+    n = sum(group[0].shape[0] for group in groups)
+    _, height, part = groups[0][0].shape
+    pieces = [piece for group in groups for piece in group]
     hbm = pl.BlockSpec(memory_space=pltpu.HBM)
     return pl.pallas_call(
-        join_kernel,
+        functools.partial(join_kernel, tuple(len(group) for group in groups)),
         grid=(1,),
         out_shape=jax.ShapeDtypeStruct((n, height, NY * part), jnp.float32),
-        in_specs=[pl.BlockSpec(memory_space=pltpu.SMEM)] + [hbm] * 5,
+        in_specs=[pl.BlockSpec(memory_space=pltpu.SMEM)] + [hbm] * len(pieces),
         out_specs=pl.BlockSpec((n, height, NY * part), lambda i: (0, 0, 0)),
-        scratch_shapes=[pltpu.SemaphoreType.DMA((5,))],
+        scratch_shapes=[pltpu.SemaphoreType.DMA((len(pieces),))],
         compiler_params=pltpu.CompilerParams(vmem_limit_bytes=24 * MIB),
         cost_estimate=pl.CostEstimate(flops=0, bytes_accessed=n * 3 * MIB, transcendentals=0),
         name="join_columns",
-    )(idx, own, *pieces)
-
-
-def assemble_kernel(idx, own, other, *refs):
-    core = idx[2]
-    out, top, low = refs[-3:]
+    )(idx, *pieces)
+
+
+def finish_kernel(idx, own, other, c, start, *refs):
+    solved, out, top, low = refs[-4:]
+    i, j = pl.program_id(0), pl.program_id(1)
     height = own.shape[1]
-    for panel in range(2):
-        value = jnp.where(core == panel, own[0], other[0])
-        rows = pl.ds(panel * height, height)
-        out[rows] = value
-        top[0, rows], low[0, rows] = split(value)
-
-
-def assemble(idx, first, own, other, solved):
+
+    @pl.when(i == 0)
+    def _():
+        for panel in range(2):
+            value = jnp.where(idx[2] == panel, own[0], other[0])
+            rows = pl.ds(panel * height, height)
+            solved[rows] = value
+            top[j, rows], low[j, rows] = split(value)
+
+    @pl.when(j == 0)
+    def _():
+        out[...] = start[...]
+
+    a_top, a_low = split(c[0])
+    out[...] -= mm3(a_top, a_low, top[j], low[j])
+
+
+def finish(idx, first, own, other, blocks, start, solved):
     n, height, columns = own.shape
+    rows = start.shape[0]
+    pair = 2 * height
+    tile = rows // 2
     hbm = pl.BlockSpec(memory_space=pltpu.HBM)
-    block = pl.BlockSpec((1, height, columns), lambda i: (i, 0, 0))
-    terms = pl.BlockSpec((1, 2 * height, columns), lambda i: (i, 0, 0))
-    term = jax.ShapeDtypeStruct((n, 2 * height, columns), jnp.bfloat16)
+
+    def once(i, j):
+        return jnp.where(i == 0, j, n - 1)
+
+    block = pl.BlockSpec((1, height, columns), lambda i, j: (once(i, j), 0, 0))
+    part = pl.BlockSpec((tile, columns), lambda i, j: (i, 0))
+    term = pltpu.VMEM((n, pair, columns), jnp.bfloat16)
     return pl.pallas_call(
-        assemble_kernel,
-        grid=(n,),
-        out_shape=[jax.ShapeDtypeStruct((NX * 2 * height, columns), jnp.float32), term, term],
-        in_specs=[pl.BlockSpec(memory_space=pltpu.SMEM), block, block] + [hbm] * len(solved),
-        out_specs=[pl.BlockSpec((2 * height, columns), lambda i: (first + i, 0)), terms, terms],
-        input_output_aliases={3: 0} if solved else {},
-        compiler_params=pltpu.CompilerParams(vmem_limit_bytes=32 * MIB),
-        cost_estimate=pl.CostEstimate(flops=0, bytes_accessed=n * 6 * MIB, transcendentals=0),
-        name="assemble_pairs",
-    )(idx, own, other, *solved)
-
-
-def product_kernel(start, c, b_top, b_low, out):
-    @pl.when(pl.program_id(1) == 0)
-    def _():
-        out[...] = start[...]
-
-    a_top, a_low = split(c[0])
-    out[...] -= mm3(a_top, a_low, b_top[0], b_low[0])
-
-
-def product(start, blocks, top, low, first):
-    rows, columns = start.shape
-    count, pair, _ = top.shape
-    tile = rows // (4 if count == 1 else 2)
-    whole = pl.BlockSpec((tile, columns), lambda i, j: (i, 0))
-    term = pl.BlockSpec((1, pair, columns), lambda i, j: (j, 0, 0))
-    return pl.pallas_call(
-        product_kernel,
-        grid=(rows // tile, count),
-        out_shape=jax.ShapeDtypeStruct(start.shape, jnp.float32),
-        in_specs=[whole, pl.BlockSpec((1, tile, pair), lambda i, j: (first + j, i, 0)), term, term],
-        out_specs=whole,
+        finish_kernel,
+        grid=(rows // tile, n),
+        out_shape=[jax.ShapeDtypeStruct((NX * pair, columns), jnp.float32), jax.ShapeDtypeStruct(start.shape, jnp.float32)],
+        in_specs=[
+            pl.BlockSpec(memory_space=pltpu.SMEM),
+            block,
+            block,
+            pl.BlockSpec((1, tile, pair), lambda i, j: (first + j, i, 0)),
+            part,
+        ]
+        + [hbm] * len(solved),
+        out_specs=[pl.BlockSpec((pair, columns), lambda i, j: (first + once(i, j), 0)), part],
+        scratch_shapes=[term, term],
+        input_output_aliases={5: 0} if solved else {},
         compiler_params=pltpu.CompilerParams(vmem_limit_bytes=40 * MIB),
         cost_estimate=pl.CostEstimate(
-            flops=6 * rows * pair * columns * count, bytes_accessed=count * 8 * MIB, transcendentals=0
+            flops=6 * n * rows * pair * columns, bytes_accessed=n * 8 * MIB, transcendentals=0
         ),
-        name="product",
-    )(start, blocks, top, low)
-
-
-def hand_kernel(filled, taken, solved, out):
+        name="finish_pairs",
+    )(idx, own, other, blocks, start, *solved)
+
+
+def hand_kernel(first, idx, filled, begin, end, taken, own, other, *refs):
+    out, rows, sems = refs[-3:]
+    before = refs[0] if len(refs) == 4 else None
     slot = pl.program_id(0)
-    count = out.shape[1]
+    core = idx[2]
+    n, height, _ = own.shape
+
+    @pl.when(slot == 0)
+    def _():
+        copies = []
+        for p in range(n):
+            for k, (src, panel) in enumerate(((own, core), (other, 1 - core))):
+                dst = rows.at[pl.ds(pl.multiple_of((2 * p + panel) * height, height), height)]
+                copies.append(pltpu.make_async_copy(src.at[p], dst, sems.at[2 * p + k]))
+        for cp in copies:
+            cp.start()
+        for cp in copies:
+            cp.wait()
+
+    out[...] = jnp.zeros_like(out) if before is None else before[...]
 
     @pl.when(filled[slot] == 1)
     def _():
-        def body(n, carry):
+        def one(i, carry):
+            out[0, pl.ds(i, 1)] = rows[pl.ds(taken[slot, i] - first * 2 * height, 1)]
+            return carry
+
+        def eight(m, carry):
             for u in range(8):
-                i = n * 8 + u
-                out[0, pl.ds(i, 1)] = solved[pl.ds(taken[slot, i], 1)]
+                one(begin[slot] + m * 8 + u, 0)
             return carry
 
-        lax.fori_loop(0, count // 8, body, 0)
-
-    @pl.when(filled[slot] == 0)
-    def _():
-        out[...] = jnp.zeros_like(out)
-
-
-def hand(filled, taken, solved):
+        whole = lax.div(end[slot] - begin[slot], 8)
+        lax.fori_loop(0, whole, eight, 0)
+        lax.fori_loop(begin[slot] + whole * 8, end[slot], one, 0)
+
+
+def hand(first, idx, filled, begin, end, taken, own, other, before):
     slots, count = taken.shape
-    columns = solved.shape[1]
+    n, height, columns = own.shape
     smem = pl.BlockSpec(memory_space=pltpu.SMEM)
+    hbm = pl.BlockSpec(memory_space=pltpu.HBM)
+    slab = pl.BlockSpec((1, count, columns), lambda i: (i, 0, 0))
     return pl.pallas_call(
-        hand_kernel,
+        functools.partial(hand_kernel, first),
         grid=(slots,),
         out_shape=jax.ShapeDtypeStruct((slots, count, columns), jnp.float32),
-        in_specs=[smem, smem, pl.BlockSpec(solved.shape, lambda i: (0, 0))],
-        out_specs=pl.BlockSpec((1, count, columns), lambda i: (i, 0, 0)),
+        in_specs=[smem] * 5 + [hbm, hbm] + [slab] * len(before),
+        out_specs=slab,
+        scratch_shapes=[pltpu.VMEM((n * 2 * height, columns), jnp.float32), pltpu.SemaphoreType.DMA((2 * n,))],
+        input_output_aliases={7: 0} if before else {},
         compiler_params=pltpu.CompilerParams(vmem_limit_bytes=32 * MIB),
-        cost_estimate=pl.CostEstimate(flops=0, bytes_accessed=10 * MIB, transcendentals=0),
+        cost_estimate=pl.CostEstimate(flops=0, bytes_accessed=n * 4 * MIB, transcendentals=0),
         name="hand_down",
-    )(filled, taken, solved)
+    )(idx, filled, begin, end, taken, own, other, *before)
 
 
 def on_device(trailing, inverse_rows, rhs_tail, coupling, rhs_head, child_rows, owner):
@@ -339,23 +360,12 @@
             first, _ = lax.optimization_barrier((halves[2:], r_own))
             first = jnp.stack(first)
             first_pieces = exchange_y(first, axis=1)
-        if p == 1:
-            second, _ = lax.optimization_barrier((halves[1][None], r_own))
-            second_pieces = exchange_y(second, axis=1)
-    first_pieces, second_pieces, last = lax.optimization_barrier((first_pieces, second_pieces, halves[0][None]))
-    last_pieces = neighbours_y(last)
-    first = join(idx, first, first_pieces)
-    solved, top, low = assemble(idx, 2, first, both_cores(first), ())
-    second = join(idx, second, second_pieces)
-    solved, top2, low2 = assemble(idx, 1, second, both_cores(second), (solved,))
-    top, last_pieces = lax.optimization_barrier((top, last_pieces))
-    last_pieces = pass_on_y(*last_pieces, 1)
-    remaining = product(rhs_head, gathered, top, low, 2)
-    remaining = product(remaining, gathered, top2, low2, 1)
-    last_pieces, remaining = lax.optimization_barrier((last_pieces, remaining))
-    last = join(idx, last, last_pieces)
-    solved, top, low = assemble(idx, 0, last, both_cores(last), (solved,))
-    remaining = product(remaining, gathered, top, low, 0)
+    last = jnp.stack(halves[:2])
+    first_pieces, last = lax.optimization_barrier((first_pieces, last))
+    last_pieces = [lax.ppermute(last, "y", [(i, i ^ s) for i in range(NY)]) for s in (2, 1, 3)]
+    last_pieces = [last_pieces[n] for n in (1, 2, 0)]
+    early = join(idx, (first, *first_pieces))
+    early_other = both_cores(early)
 
     group = (x * NY + y) * NC + core
     owned = (owner == group).astype(jnp.int32)
@@ -364,7 +374,17 @@
     picked = (owned[None, :] == 1) & (rank[None, :] == slot_ids[:, None])
     rows_taken = jnp.sum(jnp.where(picked[:, :, None], child_rows[None, :, :], 0), axis=1)
     filled = jnp.any(picked, axis=1)
-    handed = hand(filled.astype(jnp.int32), rows_taken, solved)
+    filled = filled.astype(jnp.int32)
+    begin = jnp.sum((rows_taken < 2 * pair).astype(jnp.int32), axis=1)
+    handed = hand(2, idx, filled, begin, jnp.full_like(begin, rows_taken.shape[1]), rows_taken, early, early_other, ())
+
+    early, early_other, handed = lax.optimization_barrier((early, early_other, handed))
+    solved, remaining = finish(idx, 2, early, early_other, gathered, rhs_head, ())
+    last_pieces, remaining = lax.optimization_barrier((last_pieces, remaining))
+    last = join(idx, (last, *last_pieces))
+    last_other = both_cores(last)
+    handed = hand(0, idx, filled, jnp.zeros_like(begin), begin, rows_taken, last, last_other, (handed,))
+    solved, remaining = finish(idx, 0, last, last_other, gathered, remaining, (solved,))
     return (remaining, solved, handed)
 
 

time: 225 us -> 211 us (0.938)
  local copies, waits for them, and re-layouts: 25.6 us -> 13.2 us
  waiting for transfers between devices: 42.3 us -> 51.2 us
  starting transfers between devices: 47.2 us -> 39.9 us
    unnamed x57 -> x27, local copies, waits for them, and re-layouts: 12.4 us -> 3.69 us
    ppermute x12, waiting for transfers between devices: 14.3 us -> 20 us  [on_device(): got = [lax.ppermute(mine, 'x', [(p, (p + s) % NX)]) for s in (2, 3, 1)]]
    all_gather x1, waiting for transfers between devices: 0.01 us -> 4.59 us  [on_device(): gathered = lax.all_gather(coupling, 'z', axis=0, tiled=False)]
    ppermute x12 -> x8, starting transfers between devices: 9.16 us -> 5.34 us  [neighbours_y(): return (lax.ppermute(piece, 'y', ONE), lax.ppermute(piece, 'y', THREE))]
    ppermute x10 -> x9, starting transfers between devices: 13.2 us -> 9.72 us  [both_cores(): return lax.ppermute(own, 'core', SWAP)]
    ppermute x0 -> x3, starting transfers between devices: none -> 3.33 us  [on_device(): lax.ppermute(last, 'y', [(i, i ^ s) for i in range(NY)])]
    ppermute x10 -> x9, waiting for transfers between devices: 6.38 us -> 9.65 us  [both_cores(): return lax.ppermute(own, 'core', SWAP)]
    ppermute x6 -> x4, waiting for transfers between devices: 2.96 us -> 0.01 us  [pass_on_y(): c = lax.ppermute(lax.slice_in_dim(b, 0, n, axis=axis), 'y', ONE)]
  transfers between devices with their start and end apart: 47 -> 41, of which waited for: 19 -> 17; matrix products, arithmetic and copies ran while one was open for 9% -> 7% of each run, Pallas kernels for 17% -> 16%
where the time goes in v1:
time: 211 us; the launch traced here: 210 us
  Pallas kernels  52.2 us (25%)
  waiting for transfers between devices  51.2 us (24%)
  starting transfers between devices  39.9 us (19%)
  blocking collectives  33.2 us (16%)
  between operations  14.5 us (7%)
  local copies, waits for them, and re-layouts  13.2 us (6%)
  other arithmetic  5.31 us (3%)
    all_to_all x1, blocking collectives, on_device(): lax.all_to_all(packed, 'y', split_axis=0, concat_axis=0, tiled=True)  33.2 us
    pallas_call x2, Pallas kernels, finish(): pl.pallas_call(finish_kernel, grid=(rows // tile, n), out_shape=[jax.Shap...  22.2 us
    ppermute x12, waiting for transfers between devices, on_device(): got = [lax.ppermute(mine, 'x', [(p, (p + s) % NX)]) for s in (2, 3, 1)]  20 us
    ppermute x12, starting transfers between devices, on_device(): got = [lax.ppermute(mine, 'x', [(p, (p + s) % NX)]) for s in (2, 3, 1)]  15.3 us
    ppermute x8, waiting for transfers between devices, neighbours_y(): return (lax.ppermute(piece, 'y', ONE), lax.ppermute(piece, 'y', THREE))  14.1 us
    pallas_call x2, Pallas kernels, hand(): pl.pallas_call(functools.partial(hand_kernel, first), grid=(slots,), out_...  11.2 us
    ppermute x9, starting transfers between devices, both_cores(): return lax.ppermute(own, 'core', SWAP)  9.72 us
    ppermute x9, waiting for transfers between devices, both_cores(): return lax.ppermute(own, 'core', SWAP)  9.65 us
  transfers between devices with their start and end apart: 41, of which 17 were waited for; matrix products, arithmetic and copies ran while one was open for 7% of the time, Pallas kernels for 16%

profile of v1, /device:TPU:1, one launch (start us, length us, event | category | flops | bytes accessed | tf_op | source)
XLA Modules:
  0.0 209.5 jit_solution(7091821499112838019)
XLA Ops:
  9.9 33.2 %all_to_all.5.fac_own = f32[4,128,1152]{2,1,0:T(8,128)S(1)} all-to-all(f32[4,128,1152]{2,1,0:T(8,128)S(1)} %pad_maximum_fusion), channel_id=1, replica_groups=mesh['x'=4,'y'=4,'core'=2,'z'=4] {'y'}, dimensions={0} | all-to-all | bytes 4718592 | tf_op jit(solution)/shard_map/all_to_all | solution.py:338
  43.1 1.9 collective-permute-start
  44.9 1.2 fusion.5
  47.1 2.1 %collective-permute-done.fac_other = f32[4,128,1152]{2,1,0:T(8,128)} collective-permute-done((f32[4,128,1152]{2,1,0:T(8,128)S(1)}, f32[4,128,1152]{2,1,0:T(8,128)}, u32[]{:S(2)}, u32[]{:S(2)}) %collective-permute-start) | collective-permute-done | bytes 2359328 | tf_op jit(solution)/shard_map/ppermute | solution.py:53
  50.8 1.4 collective-permute-start.1
  52.2 1.4 collective-permute-start.2
  53.5 1.3 collective-permute-start.3
  54.9 6.3 %collective-permute-done.6.far = f32[128,1024]{1,0:T(8,128)S(1)} collective-permute-done((f32[128,1024]{1,0:T(8,128)}, f32[128,1024]{1,0:T(8,128)S(1)}, u32[]{:S(2)}, u32[]{:S(2)}) %collective-permute-start.6) | collective-permute-done | bytes 524320 | tf_op jit(solution)/shard_map/ppermute | solution.py:60
  63.4 4.9 %collective-permute-done.3 = f32[512,128]{1,0:T(8,128)} collective-permute-done((f32[512,128]{1,0:T(8,128)S(1)}, f32[512,128]{1,0:T(8,128)}, u32[]{:S(2)}, u32[]{:S(2)}) %collective-permute-start.3) | collective-permute-done | bytes 262176 | tf_op jit(solution)/shard_map/ppermute | solution.py:353
  68.3 1.2 add_select_fusion.2.mine
  72.7 2.9 %update_rows.3.r_own = f32[4,128,128]{2,1,0:T(8,128)S(1)} custom-call(s32[4]{0:T(128)S(1)} %pad_add_fusion.idx, f32[512,128]{1,0:T(8,128)S(1)} %add_select_fusion.2.mine, f32[512,128]{1,0:T(8,128)S(1)} %collective-permute-done.4.other, f32[4,128,128]{2,1,0:T(8,128)S(1)} %slice.52.r_own, f32[128,4096]{1,0:T(8,128)S(1)} %copy-done.1, ...), custom_call_target="tpu_custom_call" | custom-call | flops 1000 | bytes 1000 | tf_op jit(solution)/shard_map/update_rows/pallas_call | solution.py:155
  76.5 1.2 collective-permute-done.9.r_other
  78.2 1.3 collective-permute-start.10
  80.2 1.4 collective-permute-start.12
  81.6 3.9 %collective-permute-done.15.far = f32[128,1024]{1,0:T(8,128)} collective-permute-done((f32[128,1024]{1,0:T(8,128)}, f32[128,1024]{1,0:T(8,128)}, u32[]{:S(2)}, u32[]{:S(2)}) %collective-permute-start.15) | collective-permute-done | bytes 524320 | tf_op jit(solution)/shard_map/ppermute | solution.py:60
  88.5 3.5 %collective-permute-done.10 = f32[512,128]{1,0:T(8,128)} collective-permute-done((f32[512,128]{1,0:T(8,128)S(1)}, f32[512,128]{1,0:T(8,128)}, u32[]{:S(2)}, u32[]{:S(2)}) %collective-permute-start.10) | collective-permute-done | bytes 262176 | tf_op jit(solution)/shard_map/ppermute | solution.py:353
  92.8 1.2 add_select_fusion.1.mine
  93.9 1.4 collective-permute-start.13
  95.4 1.3 collective-permute-start.28
  97.8 3.3 %update_rows.4.r_own = f32[4,128,128]{2,1,0:T(8,128)S(1)} custom-call(s32[4]{0:T(128)S(1)} %pad_add_fusion.idx, f32[512,128]{1,0:T(8,128)S(1)} %add_select_fusion.1.mine, f32[512,128]{1,0:T(8,128)S(1)} %collective-permute-done.13.other, f32[4,128,128]{2,1,0:T(8,128)S(1)} %update_rows.3.r_own, f32[128,4096]{1,0:T(8,128)S(1)} %copy-done.2, ...), custom_call_target="tpu_custom_call" | custom-call | flops 1000 | bytes 1000 | tf_op jit(solution)/shard_map/update_rows/pallas_call | solution.py:155
  101.8 1.2 collective-permute-done.22.r_other
  103.6 1.4 collective-permute-start.23
  105.0 1.3 collective-permute-start.24
  106.3 1.4 collective-permute-start.25
  107.6 2.8 %collective-permute-done.28.far = f32[128,1024]{1,0:T(8,128)} collective-permute-done((f32[128,1024]{1,0:T(8,128)}, f32[128,1024]{1,0:T(8,128)}, u32[]{:S(2)}, u32[]{:S(2)}) %collective-permute-start.28) | collective-permute-done | bytes 524320 | tf_op jit(solution)/shard_map/ppermute | solution.py:60
  112.4 1.8 collective-permute-start.30
  114.3 7.1 %collective-permute-done.24 = f32[512,128]{1,0:T(8,128)} collective-permute-done((f32[512,128]{1,0:T(8,128)S(1)}, f32[512,128]{1,0:T(8,128)}, u32[]{:S(2)}, u32[]{:S(2)}) %collective-permute-start.24) | collective-permute-done | bytes 262176 | tf_op jit(solution)/shard_map/ppermute | solution.py:353
  121.4 1.2 add_select_fusion.mine
  125.5 3.1 %update_rows.5.r_own = f32[4,128,128]{2,1,0:T(8,128)S(1)} custom-call(s32[4]{0:T(128)S(1)} %pad_add_fusion.idx, f32[512,128]{1,0:T(8,128)S(1)} %add_select_fusion.mine, f32[512,128]{1,0:T(8,128)S(1)} %collective-permute-done.26.other, f32[4,128,128]{2,1,0:T(8,128)S(1)} %update_rows.4.r_own, f32[128,4096]{1,0:T(8,128)S(1)} %copy-done.3, ...), custom_call_target="tpu_custom_call" | custom-call | flops 1000 | bytes 1000 | tf_op jit(solution)/shard_map/update_rows/pallas_call | solution.py:155
  130.4 3.9 %solve_pair.7 = f32[512,128]{1,0:T(8,128)S(1)} custom-call(s32[4]{0:T(128)S(1)} %pad_add_fusion.idx, f32[4,128,1152]{2,1,0:T(8,128)S(1)} %all_to_all.5.fac_own, f32[4,128,1152]{2,1,0:T(8,128)} %collective-permute-done.fac_other, f32[4,128,128]{2,1,0:T(8,128)S(1)} %update_rows.5.r_own, f32[4,128,128]{2,1,0:T(8,128)S(1)} %collective-permute-done.31.r_other), custom_call_target="tpu_custom_call" | custom-call | flops 1000 | bytes 1000 | tf_op jit(solution)/shard_map/solve_pair/pallas_call | solution.py:109
  134.4 1.3 collective-permute-start.32
  135.7 1.3 collective-permute-start.33
  137.0 1.3 collective-permute-start.34
  140.6 1.9 collective-permute-start.21
  142.6 4.3 %collective-permute-done.34 = f32[512,128]{1,0:T(8,128)S(1)} collective-permute-done((f32[512,128]{1,0:T(8,128)S(1)}, f32[512,128]{1,0:T(8,128)S(1)}, u32[]{:S(2)}, u32[]{:S(2)}) %collective-permute-start.34) | collective-permute-done | bytes 262176 | tf_op jit(solution)/shard_map/ppermute | solution.py:353
  147.0 2.2 %collective-permute-done.21.refs_4_ = f32[2,256,128]{2,1,0:T(8,128)S(1)} collective-permute-done((f32[2,256,128]{2,1,0:T(8,128)S(1)}, f32[2,256,128]{2,1,0:T(8,128)S(1)}, u32[]{:S(2)}, u32[]{:S(2)}) %collective-permute-start.21) | collective-permute-done | bytes 262176 | tf_op jit(solution)/shard_map/ppermute | solution.py:66
  149.2 1.8 join_columns.2.own
  151.0 1.5 collective-permute-start.38
  153.4 1.8 collective-permute-start.36
  155.2 1.4 collective-permute-start.37
  156.5 5.9 %hand_down.2.refs_0_ = f32[4,256,512]{2,1,0:T(8,128)} custom-call(s32[4]{0:T(128)S(1)} %pad_add_fusion.idx, s32[4]{0:T(128)S(1)} %convert_element_type.10.filled, s32[4]{0:T(128)S(1)} %convert_reduce_fusion.begin.end, s32[4]{0:T(128)S(1)} %broadcast_3_end.2.end, s32[4,256]{1,0:T(4,128)S(1)} %select_reduce_fusion.taken, f32[2,512,512]{2,1,0:T(8,128)S(1)} %join_columns.2.own, ...), custom_call_target="tpu_custom_call" | custom-call | bytes 8388608 | tf_op jit(solution)/shard_map/hand_down/pallas_call | solution.py:306
  162.5 4.6 %all-gather.3.cloned.1.call-done = f32[4096,1024]{1,0:T(8,128)} async-done(((f32[1024,1024]{1,0:T(8,128)}), f32[4096,1024]{1,0:T(8,128)}) %all-gather.3.cloned.1.call-update) | async-done | bytes 16777232 | tf_op jit(solution)/shard_map/all_gather | solution.py:332
  167.1 1.6 copy-done.7
  168.7 11.1 %finish_pairs.2 = (f32[4096,512]{1,0:T(8,128)}, f32[1024,512]{1,0:T(8,128)S(1)}) custom-call(s32[4]{0:T(128)S(1)} %pad_add_fusion.idx, f32[2,512,512]{2,1,0:T(8,128)S(1)} %join_columns.2.own, f32[2,512,512]{2,1,0:T(8,128)} %collective-permute-done.38.other, f32[4,1024,1024]{2,1,0:T(8,128)} %bitcast.17, f32[1024,512]{1,0:T(8,128)S(1)} %copy-done.7), custom_call_target="tpu_custom_call" | custom-call | flops 6442450944 | bytes 16777216 | tf_op jit(solution)/shard_map/finish_pairs/pallas_call | solution.py:240
  179.8 1.9 join_columns.3.own
  182.5 3.8 %collective-permute-done.39.other = f32[2,512,512]{2,1,0:T(8,128)S(1)} collective-permute-done((f32[2,512,512]{2,1,0:T(8,128)S(1)}, f32[2,512,512]{2,1,0:T(8,128)S(1)}, u32[]{:S(2)}, u32[]{:S(2)}) %collective-permute-start.39) | collective-permute-done | bytes 2097184 | tf_op jit(solution)/shard_map/ppermute | solution.py:53
  186.3 5.2 %hand_down.3 = f32[4,256,512]{2,1,0:T(8,128)} custom-call(s32[4]{0:T(128)S(1)} %pad_add_fusion.idx, s32[4]{0:T(128)S(1)} %convert_element_type.10.filled, s32[4]{0:T(128)S(1)} %broadcast_2_begin.2.begin, s32[4]{0:T(128)S(1)} %convert_reduce_fusion.begin.end, s32[4,256]{1,0:T(4,128)S(1)} %select_reduce_fusion.taken, ...), custom_call_target="tpu_custom_call", output_to_operand_aliasing={{}: (7, {})} | custom-call | bytes 8388608 | tf_op jit(solution)/shard_map/hand_down/pallas_call | solution.py:306
  191.5 11.2 %finish_pairs.3 = (f32[4096,512]{1,0:T(8,128)}, f32[1024,512]{1,0:T(8,128)}) custom-call(s32[4]{0:T(128)S(1)} %pad_add_fusion.idx, f32[2,512,512]{2,1,0:T(8,128)S(1)} %join_columns.3.own, f32[2,512,512]{2,1,0:T(8,128)S(1)} %collective-permute-done.39.other, f32[4,1024,1024]{2,1,0:T(8,128)} %bitcast.18, ...), custom_call_target="tpu_custom_call", output_to_operand_aliasing={{0}: (5, {})} | custom-call | flops 6442450944 | bytes 16777216 | tf_op jit(solution)/shard_map/finish_pairs/pallas_call | solution.py:240
  (110 shorter events, 29.8 us)
Async XLA Ops:
  7.2 159.9 %all-gather.3.cloned.1.call-start = ((), (), s32[]{:S(2)}) async-start(), calls=%async_computation.1 | async-start | bytes 20971520 | tf_op jit(solution)/shard_map/all_gather | solution.py:332
  9.9 35.1 %copy-start = (f32[128,4096]{1,0:T(8,128)S(1)}, f32[128,4096]{1,0:T(8,128)}, u32[]{:S(2)}) copy-start(f32[128,4096]{1,0:T(8,128)} %trailing.5) | copy-start | bytes 6291460
  43.1 6.2 %collective-permute-start = (f32[4,128,1152]{2,1,0:T(8,128)S(1)}, f32[4,128,1152]{2,1,0:T(8,128)}, u32[]{:S(2)}, u32[]{:S(2)}) collective-permute-start(f32[4,128,1152]{2,1,0:T(8,128)S(1)} %all_to_all.5.fac_own), channel_id=1, source_target_pairs={{0,4},{4,0},{1,5},{5,1},{2,6},{6,2},{3,7},{7,3},{8,12},{12,8},{9,1... | collective-permute-start | bytes 7077896 | tf_op jit(solution)/shard_map/ppermute | solution.py:53
  46.1 15.1 %collective-permute-start.6 = (f32[128,1024]{1,0:T(8,128)}, f32[128,1024]{1,0:T(8,128)S(1)}, u32[]{:S(2)}, u32[]{:S(2)}) collective-permute-start(f32[128,1024]{1,0:T(8,128)} %get-tuple-element.24), channel_id=1, source_target_pairs={{0,24},{8,16},{16,8},{24,0},{1,25},{9,17},{17,9},{25,1},{2,26},{10... | collective-permute-start | bytes 1572872 | tf_op jit(solution)/shard_map/ppermute | solution.py:60
  47.0 14.3 %collective-permute-start.5 = (f32[128,1024]{1,0:T(8,128)}, f32[128,1024]{1,0:T(8,128)}, u32[]{:S(2)}, u32[]{:S(2)}) collective-permute-start(f32[128,1024]{1,0:T(8,128)} %get-tuple-element.24), channel_id=1, source_target_pairs={{0,8},{8,0},{16,24},{24,16},{1,9},{9,1},{17,25},{25,17},{2,10},{10... | collective-permute-start | bytes 1572872 | tf_op jit(solution)/shard_map/ppermute | solution.py:60
  50.8 12.6 %collective-permute-start.1 = (f32[512,128]{1,0:T(8,128)S(1)}, f32[512,128]{1,0:T(8,128)}, u32[]{:S(2)}, u32[]{:S(2)}) collective-permute-start(f32[512,128]{1,0:T(8,128)S(1)} %solve_pair.4), channel_id=1, source_target_pairs={{96,32},{97,33},{98,34},{99,35},{100,36},{101,37},{102,38},{103,39... | collective-permute-start | bytes 786440 | tf_op jit(solution)/shard_map/ppermute | solution.py:353
  52.2 11.2 %collective-permute-start.2 = (f32[512,128]{1,0:T(8,128)S(1)}, f32[512,128]{1,0:T(8,128)}, u32[]{:S(2)}, u32[]{:S(2)}) collective-permute-start(f32[512,128]{1,0:T(8,128)S(1)} %solve_pair.4), channel_id=1, source_target_pairs={{96,64},{97,65},{98,66},{99,67},{100,68},{101,69},{102,70},{103,71... | collective-permute-start | bytes 786440 | tf_op jit(solution)/shard_map/ppermute | solution.py:353
  53.5 14.8 %collective-permute-start.3 = (f32[512,128]{1,0:T(8,128)S(1)}, f32[512,128]{1,0:T(8,128)}, u32[]{:S(2)}, u32[]{:S(2)}) collective-permute-start(f32[512,128]{1,0:T(8,128)S(1)} %solve_pair.4), channel_id=1, source_target_pairs={{96,0},{97,1},{98,2},{99,3},{100,4},{101,5},{102,6},{103,7},{104,8... | collective-permute-start | bytes 786440 | tf_op jit(solution)/shard_map/ppermute | solution.py:353
  54.8 16.8 %copy-start.1 = (f32[128,4096]{1,0:T(8,128)S(1)}, f32[128,4096]{1,0:T(8,128)}, u32[]{:S(2)}) copy-start(f32[128,4096]{1,0:T(8,128)} %trailing.5) | copy-start | bytes 6291460
  61.2 10.2 %collective-permute-start.7 = (f32[64,1024]{1,0:T(8,128)S(1)}, f32[64,1024]{1,0:T(8,128)S(1)}, u32[]{:S(2)}, u32[]{:S(2)}) collective-permute-start(f32[64,1024]{1,0:T(8,128)S(1)} %slice.54), channel_id=1, source_target_pairs={{0,8},{8,0},{16,24},{24,16},{1,9},{9,1},{17,25},{25,17},{2,10},{10... | collective-permute-start | bytes 786440 | tf_op jit(solution)/shard_map/ppermute | solution.py:65
  62.4 9.0 %collective-permute-start.8 = (f32[64,1024]{1,0:T(8,128)S(1)}, f32[64,1024]{1,0:T(8,128)S(1)}, u32[]{:S(2)}, u32[]{:S(2)}) collective-permute-start(f32[64,1024]{1,0:T(8,128)S(1)} %slice.55), channel_id=1, source_target_pairs={{0,24},{8,16},{16,8},{24,0},{1,25},{9,17},{17,9},{25,1},{2,26},{10... | collective-permute-start | bytes 786440 | tf_op jit(solution)/shard_map/ppermute | solution.py:66
  69.5 2.1 %collective-permute-start.4 = (f32[512,128]{1,0:T(8,128)S(1)}, f32[512,128]{1,0:T(8,128)S(1)}, u32[]{:S(2)}, u32[]{:S(2)}) collective-permute-start(f32[512,128]{1,0:T(8,128)S(1)} %add_select_fusion.2.mine), channel_id=1, source_target_pairs={{0,4},{4,0},{1,5},{5,1},{2,6},{6,2},{3,7},{7,3},{8,12},{12,8},{9,1... | collective-permute-start | bytes 786440 | tf_op jit(solution)/shard_map/ppermute | solution.py:53
  70.5 15.0 %collective-permute-start.15 = (f32[128,1024]{1,0:T(8,128)}, f32[128,1024]{1,0:T(8,128)}, u32[]{:S(2)}, u32[]{:S(2)}) collective-permute-start(f32[128,1024]{1,0:T(8,128)} %get-tuple-element.25), channel_id=1, source_target_pairs={{0,24},{8,16},{16,8},{24,0},{1,25},{9,17},{17,9},{25,1},{2,26},{10... | collective-permute-start | bytes 1572872 | tf_op jit(solution)/shard_map/ppermute | solution.py:60
  71.4 15.2 %collective-permute-start.14 = (f32[128,1024]{1,0:T(8,128)}, f32[128,1024]{1,0:T(8,128)}, u32[]{:S(2)}, u32[]{:S(2)}) collective-permute-start(f32[128,1024]{1,0:T(8,128)} %get-tuple-element.25), channel_id=1, source_target_pairs={{0,8},{8,0},{16,24},{24,16},{1,9},{9,1},{17,25},{25,17},{2,10},{10... | collective-permute-start | bytes 1572872 | tf_op jit(solution)/shard_map/ppermute | solution.py:60
  75.6 2.0 collective-permute-start.9
  78.2 13.8 %collective-permute-start.10 = (f32[512,128]{1,0:T(8,128)S(1)}, f32[512,128]{1,0:T(8,128)}, u32[]{:S(2)}, u32[]{:S(2)}) collective-permute-start(f32[512,128]{1,0:T(8,128)S(1)} %solve_pair.5), channel_id=1, source_target_pairs={{64,0},{65,1},{66,2},{67,3},{68,4},{69,5},{70,6},{71,7},{72,8},{73... | collective-permute-start | bytes 786440 | tf_op jit(solution)/shard_map/ppermute | solution.py:353
  79.5 12.5 %collective-permute-start.11 = (f32[512,128]{1,0:T(8,128)S(1)}, f32[512,128]{1,0:T(8,128)S(1)}, u32[]{:S(2)}, u32[]{:S(2)}) collective-permute-start(f32[512,128]{1,0:T(8,128)S(1)} %solve_pair.5), channel_id=1, source_target_pairs={{64,32},{65,33},{66,34},{67,35},{68,36},{69,37},{70,38},{71,39},{7... | collective-permute-start | bytes 786440 | tf_op jit(solution)/shard_map/ppermute | solution.py:353
  80.2 12.5 %collective-permute-start.12 = (f32[512,128]{1,0:T(8,128)S(1)}, f32[512,128]{1,0:T(8,128)}, u32[]{:S(2)}, u32[]{:S(2)}) collective-permute-start(f32[512,128]{1,0:T(8,128)S(1)} %solve_pair.5), channel_id=1, source_target_pairs={{64,96},{65,97},{66,98},{67,99},{68,100},{69,101},{70,102},{71,103... | collective-permute-start | bytes 786440 | tf_op jit(solution)/shard_map/ppermute | solution.py:353
  81.6 16.2 %copy-start.2 = (f32[128,4096]{1,0:T(8,128)S(1)}, f32[128,4096]{1,0:T(8,128)}, u32[]{:S(2)}) copy-start(f32[128,4096]{1,0:T(8,128)} %trailing.5) | copy-start | bytes 6291460
  86.5 11.3 %collective-permute-start.16 = (f32[64,1024]{1,0:T(8,128)S(1)}, f32[64,1024]{1,0:T(8,128)S(1)}, u32[]{:S(2)}, u32[]{:S(2)}) collective-permute-start(f32[64,1024]{1,0:T(8,128)S(1)} %slice.56), channel_id=1, source_target_pairs={{0,8},{8,0},{16,24},{24,16},{1,9},{9,1},{17,25},{25,17},{2,10},{10... | collective-permute-start | bytes 786440 | tf_op jit(solution)/shard_map/ppermute | solution.py:65
  87.5 10.3 %collective-permute-start.17 = (f32[64,1024]{1,0:T(8,128)S(1)}, f32[64,1024]{1,0:T(8,128)S(1)}, u32[]{:S(2)}, u32[]{:S(2)}) collective-permute-start(f32[64,1024]{1,0:T(8,128)S(1)} %slice.57), channel_id=1, source_target_pairs={{0,24},{8,16},{16,8},{24,0},{1,25},{9,17},{17,9},{25,1},{2,26},{10... | collective-permute-start | bytes 786440 | tf_op jit(solution)/shard_map/ppermute | solution.py:66
  93.9 3.9 %collective-permute-start.13 = (f32[512,128]{1,0:T(8,128)S(1)}, f32[512,128]{1,0:T(8,128)S(1)}, u32[]{:S(2)}, u32[]{:S(2)}) collective-permute-start(f32[512,128]{1,0:T(8,128)S(1)} %add_select_fusion.1.mine), channel_id=1, source_target_pairs={{0,4},{4,0},{1,5},{5,1},{2,6},{6,2},{3,7},{7,3},{8,12},{12,8},{9,1... | collective-permute-start | bytes 786440 | tf_op jit(solution)/shard_map/ppermute | solution.py:53
  95.4 15.0 %collective-permute-start.28 = (f32[128,1024]{1,0:T(8,128)}, f32[128,1024]{1,0:T(8,128)}, u32[]{:S(2)}, u32[]{:S(2)}) collective-permute-start(f32[128,1024]{1,0:T(8,128)} %get-tuple-element.28), channel_id=1, source_target_pairs={{0,24},{8,16},{16,8},{24,0},{1,25},{9,17},{17,9},{25,1},{2,26},{10... | collective-permute-start | bytes 1572872 | tf_op jit(solution)/shard_map/ppermute | solution.py:60
  96.7 14.8 %collective-permute-start.27 = (f32[128,1024]{1,0:T(8,128)}, f32[128,1024]{1,0:T(8,128)}, u32[]{:S(2)}, u32[]{:S(2)}) collective-permute-start(f32[128,1024]{1,0:T(8,128)} %get-tuple-element.28), channel_id=1, source_target_pairs={{0,8},{8,0},{16,24},{24,16},{1,9},{9,1},{17,25},{25,17},{2,10},{10... | collective-permute-start | bytes 1572872 | tf_op jit(solution)/shard_map/ppermute | solution.py:60
  101.1 1.9 collective-permute-start.22
  103.6 17.8 %copy-start.6 = (f32[512,128]{1,0:T(8,128)}, f32[512,128]{1,0:T(8,128)S(1)}, u32[]{:S(2)}) copy-start(f32[512,128]{1,0:T(8,128)S(1)} %solve_pair.6) | copy-start | bytes 786436
  103.6 10.7 %collective-permute-start.23 = (f32[512,128]{1,0:T(8,128)S(1)}, f32[512,128]{1,0:T(8,128)}, u32[]{:S(2)}, u32[]{:S(2)}) collective-permute-start(f32[512,128]{1,0:T(8,128)S(1)} %solve_pair.6), channel_id=1, source_target_pairs={{32,96},{33,97},{34,98},{35,99},{36,100},{37,101},{38,102},{39,103... | collective-permute-start | bytes 786440 | tf_op jit(solution)/shard_map/ppermute | solution.py:353
  105.0 16.4 %collective-permute-start.24 = (f32[512,128]{1,0:T(8,128)S(1)}, f32[512,128]{1,0:T(8,128)}, u32[]{:S(2)}, u32[]{:S(2)}) collective-permute-start(f32[512,128]{1,0:T(8,128)S(1)} %solve_pair.6), channel_id=1, source_target_pairs={{32,0},{33,1},{34,2},{35,3},{36,4},{37,5},{38,6},{39,7},{40,8},{41... | collective-permute-start | bytes 786440 | tf_op jit(solution)/shard_map/ppermute | solution.py:353
  106.3 15.1 %collective-permute-start.25 = (f32[512,128]{1,0:T(8,128)S(1)}, f32[512,128]{1,0:T(8,128)}, u32[]{:S(2)}, u32[]{:S(2)}) collective-permute-start(f32[512,128]{1,0:T(8,128)S(1)} %solve_pair.6), channel_id=1, source_target_pairs={{32,64},{33,65},{34,66},{35,67},{36,68},{37,69},{38,70},{39,71},{4... | collective-permute-start | bytes 786440 | tf_op jit(solution)/shard_map/ppermute | solution.py:353
  107.6 17.9 %copy-start.3 = (f32[128,4096]{1,0:T(8,128)S(1)}, f32[128,4096]{1,0:T(8,128)}, u32[]{:S(2)}) copy-start(f32[128,4096]{1,0:T(8,128)} %trailing.5) | copy-start | bytes 6291460
  111.4 14.1 %collective-permute-start.29 = (f32[64,1024]{1,0:T(8,128)S(1)}, f32[64,1024]{1,0:T(8,128)S(1)}, u32[]{:S(2)}, u32[]{:S(2)}) collective-permute-start(f32[64,1024]{1,0:T(8,128)S(1)} %slice.60), channel_id=1, source_target_pairs={{0,8},{8,0},{16,24},{24,16},{1,9},{9,1},{17,25},{25,17},{2,10},{10... | collective-permute-start | bytes 786440 | tf_op jit(solution)/shard_map/ppermute | solution.py:65
  112.4 13.0 %collective-permute-start.30 = (f32[64,1024]{1,0:T(8,128)S(1)}, f32[64,1024]{1,0:T(8,128)S(1)}, u32[]{:S(2)}, u32[]{:S(2)}) collective-permute-start(f32[64,1024]{1,0:T(8,128)S(1)} %slice.61), channel_id=1, source_target_pairs={{0,24},{8,16},{16,8},{24,0},{1,25},{9,17},{17,9},{25,1},{2,26},{10... | collective-permute-start | bytes 786440 | tf_op jit(solution)/shard_map/ppermute | solution.py:66
  122.5 2.9 %collective-permute-start.26 = (f32[512,128]{1,0:T(8,128)S(1)}, f32[512,128]{1,0:T(8,128)S(1)}, u32[]{:S(2)}, u32[]{:S(2)}) collective-permute-start(f32[512,128]{1,0:T(8,128)S(1)} %add_select_fusion.mine), channel_id=1, source_target_pairs={{0,4},{4,0},{1,5},{5,1},{2,6},{6,2},{3,7},{7,3},{8,12},{12,8},{9,1... | collective-permute-start | bytes 786440 | tf_op jit(solution)/shard_map/ppermute | solution.py:53
  124.3 15.1 %collective-permute-start.19 = (f32[2,512,128]{2,1,0:T(8,128)}, f32[2,512,128]{2,1,0:T(8,128)S(1)}, u32[]{:S(2)}, u32[]{:S(2)}) collective-permute-start(f32[2,512,128]{2,1,0:T(8,128)} %pad_maximum_fusion.2.refs_0_), channel_id=1, source_target_pairs={{0,24},{8,16},{16,8},{24,0},{1,25},{9,17},{17,9},{25,1},{2,26},{10... | collective-permute-start | bytes 1572872 | tf_op jit(solution)/shard_map/ppermute | solution.py:60
  125.2 14.4 %collective-permute-start.18 = (f32[2,512,128]{2,1,0:T(8,128)}, f32[2,512,128]{2,1,0:T(8,128)}, u32[]{:S(2)}, u32[]{:S(2)}) collective-permute-start(f32[2,512,128]{2,1,0:T(8,128)} %pad_maximum_fusion.2.refs_0_), channel_id=1, source_target_pairs={{0,8},{8,0},{16,24},{24,16},{1,9},{9,1},{17,25},{25,17},{2,10},{10... | collective-permute-start | bytes 1572872 | tf_op jit(solution)/shard_map/ppermute | solution.py:60
  128.6 1.8 collective-permute-start.31
  134.4 8.1 %collective-permute-start.32 = (f32[512,128]{1,0:T(8,128)S(1)}, f32[512,128]{1,0:T(8,128)S(1)}, u32[]{:S(2)}, u32[]{:S(2)}) collective-permute-start(f32[512,128]{1,0:T(8,128)S(1)} %solve_pair.7), channel_id=1, source_target_pairs={{0,64},{1,65},{2,66},{3,67},{4,68},{5,69},{6,70},{7,71},{8,72},{9,... | collective-permute-start | bytes 786440 | tf_op jit(solution)/shard_map/ppermute | solution.py:353
  135.7 6.9 %collective-permute-start.33 = (f32[512,128]{1,0:T(8,128)S(1)}, f32[512,128]{1,0:T(8,128)S(1)}, u32[]{:S(2)}, u32[]{:S(2)}) collective-permute-start(f32[512,128]{1,0:T(8,128)S(1)} %solve_pair.7), channel_id=1, source_target_pairs={{0,96},{1,97},{2,98},{3,99},{4,100},{5,101},{6,102},{7,103},{8,104... | collective-permute-start | bytes 786440 | tf_op jit(solution)/shard_map/ppermute | solution.py:353
  137.0 9.9 %collective-permute-start.34 = (f32[512,128]{1,0:T(8,128)S(1)}, f32[512,128]{1,0:T(8,128)S(1)}, u32[]{:S(2)}, u32[]{:S(2)}) collective-permute-start(f32[512,128]{1,0:T(8,128)S(1)} %solve_pair.7), channel_id=1, source_target_pairs={{0,32},{1,33},{2,34},{3,35},{4,36},{5,37},{6,38},{7,39},{8,40},{9,... | collective-permute-start | bytes 786440 | tf_op jit(solution)/shard_map/ppermute | solution.py:353
  139.4 7.6 %collective-permute-start.20 = (f32[2,256,128]{2,1,0:T(8,128)S(1)}, f32[2,256,128]{2,1,0:T(8,128)S(1)}, u32[]{:S(2)}, u32[]{:S(2)}) collective-permute-start(f32[2,256,128]{2,1,0:T(8,128)S(1)} %slice.58), channel_id=1, source_target_pairs={{0,8},{8,0},{16,24},{24,16},{1,9},{9,1},{17,25},{25,17},{2,10},{10... | collective-permute-start | bytes 786440 | tf_op jit(solution)/shard_map/ppermute | solution.py:65
  140.6 8.6 %collective-permute-start.21 = (f32[2,256,128]{2,1,0:T(8,128)S(1)}, f32[2,256,128]{2,1,0:T(8,128)S(1)}, u32[]{:S(2)}, u32[]{:S(2)}) collective-permute-start(f32[2,256,128]{2,1,0:T(8,128)S(1)} %slice.59), channel_id=1, source_target_pairs={{0,24},{8,16},{16,8},{24,0},{1,25},{9,17},{17,9},{25,1},{2,26},{10... | collective-permute-start | bytes 786440 | tf_op jit(solution)/shard_map/ppermute | solution.py:66
  147.0 5.5 %copy-start.12 = (s32[64]{0:T(128)S(1)}, s32[64]{0:T(128)}, u32[]{:S(2)}) copy-start(s32[64]{0:T(128)} %param.13) | copy-start | bytes 772
  147.0 6.0 %copy-start.11 = (s32[64,256]{1,0:T(8,128)S(1)}, s32[64,256]{1,0:T(8,128)}, u32[]{:S(2)}) copy-start(s32[64,256]{1,0:T(8,128)} %param.12) | copy-start | bytes 196612
  151.0 5.5 %collective-permute-start.38 = (f32[2,512,512]{2,1,0:T(8,128)S(1)}, f32[2,512,512]{2,1,0:T(8,128)}, u32[]{:S(2)}, u32[]{:S(2)}) collective-permute-start(f32[2,512,512]{2,1,0:T(8,128)S(1)} %join_columns.2.own), channel_id=1, source_target_pairs={{0,4},{4,0},{1,5},{5,1},{2,6},{6,2},{3,7},{7,3},{8,12},{12,8},{9,1... | collective-permute-start | bytes 6291464 | tf_op jit(solution)/shard_map/ppermute | solution.py:53
  153.2 26.5 %collective-permute-start.35 = (f32[2,512,128]{2,1,0:T(8,128)S(1)}, f32[2,512,128]{2,1,0:T(8,128)S(1)}, u32[]{:S(2)}, u32[]{:S(2)}) collective-permute-start(f32[2,512,128]{2,1,0:T(8,128)S(1)} %pad_maximum_fusion.3.refs_0_), channel_id=1, source_target_pairs={{0,8},{8,0},{16,24},{24,16},{1,9},{9,1},{17,25},{25,17},{2,10},{10... | collective-permute-start | bytes 1572872 | tf_op jit(solution)/shard_map/ppermute | solution.py:365
  153.4 26.3 %collective-permute-start.36 = (f32[2,512,128]{2,1,0:T(8,128)S(1)}, f32[2,512,128]{2,1,0:T(8,128)}, u32[]{:S(2)}, u32[]{:S(2)}) collective-permute-start(f32[2,512,128]{2,1,0:T(8,128)S(1)} %pad_maximum_fusion.3.refs_0_), channel_id=1, source_target_pairs={{0,24},{8,16},{16,8},{24,0},{1,25},{9,17},{17,9},{25,1},{2,26},{10... | collective-permute-start | bytes 1572872 | tf_op jit(solution)/shard_map/ppermute | solution.py:365
  155.2 24.6 %collective-permute-start.37 = (f32[2,512,128]{2,1,0:T(8,128)S(1)}, f32[2,512,128]{2,1,0:T(8,128)}, u32[]{:S(2)}, u32[]{:S(2)}) collective-permute-start(f32[2,512,128]{2,1,0:T(8,128)S(1)} %pad_maximum_fusion.3.refs_0_), channel_id=1, source_target_pairs={{0,16},{8,24},{16,0},{24,8},{1,17},{9,25},{17,1},{25,9},{2,18},{10... | collective-permute-start | bytes 1572872 | tf_op jit(solution)/shard_map/ppermute | solution.py:365
  181.7 4.6 %collective-permute-start.39 = (f32[2,512,512]{2,1,0:T(8,128)S(1)}, f32[2,512,512]{2,1,0:T(8,128)S(1)}, u32[]{:S(2)}, u32[]{:S(2)}) collective-permute-start(f32[2,512,512]{2,1,0:T(8,128)S(1)} %join_columns.3.own), channel_id=1, source_target_pairs={{0,4},{4,0},{1,5},{5,1},{2,6},{6,2},{3,7},{7,3},{8,12},{12,8},{9,1... | collective-permute-start | bytes 6291464 | tf_op jit(solution)/shard_map/ppermute | solution.py:53
  (6 other events, 8.7 us)
Sparse Core Ops, SparseCore 0:
  9.7 157.3 all-gather.2

commit v2 on v1

--- a/solution.py
+++ b/solution.py
@@ -112,7 +112,7 @@
         in_specs=[pl.BlockSpec(memory_space=pltpu.SMEM), hbm, hbm, vmem, vmem],
         out_specs=vmem,
         scratch_shapes=[half, half, half, pltpu.SemaphoreType.DMA((6,))],
-        compiler_params=pltpu.CompilerParams(vmem_limit_bytes=24 * MIB),
+        compiler_params=pltpu.CompilerParams(vmem_limit_bytes=16 * MIB),
         cost_estimate=pl.CostEstimate(flops=1000, bytes_accessed=1000, transcendentals=0),
         name="solve_pair",
     )(idx, packed, packed_other, r_own, r_other)
@@ -158,7 +158,7 @@
         in_specs=[pl.BlockSpec(memory_space=pltpu.SMEM), vmem, vmem, vmem] + [hbm] * 5,
         out_specs=vmem,
         scratch_shapes=[pltpu.VMEM((NY, rows, pair), jnp.float32), pltpu.SemaphoreType.DMA((5,))],
-        compiler_params=pltpu.CompilerParams(vmem_limit_bytes=24 * MIB),
+        compiler_params=pltpu.CompilerParams(vmem_limit_bytes=16 * MIB),
         cost_estimate=pl.CostEstimate(flops=1000, bytes_accessed=1000, transcendentals=0),
         name="update_rows",
     )(idx, mine, other, r_own, trailing, *pieces)
@@ -197,13 +197,14 @@
         in_specs=[pl.BlockSpec(memory_space=pltpu.SMEM)] + [hbm] * len(pieces),
         out_specs=pl.BlockSpec((n, height, NY * part), lambda i: (0, 0, 0)),
         scratch_shapes=[pltpu.SemaphoreType.DMA((len(pieces),))],
-        compiler_params=pltpu.CompilerParams(vmem_limit_bytes=24 * MIB),
+        compiler_params=pltpu.CompilerParams(vmem_limit_bytes=12 * MIB),
         cost_estimate=pl.CostEstimate(flops=0, bytes_accessed=n * 3 * MIB, transcendentals=0),
         name="join_columns",
     )(idx, *pieces)
 
 
-def finish_kernel(idx, own, other, c, start, *refs):
+def finish_kernel(count, idx, own, other, c, *refs):
+    starts = refs[:count]
     solved, out, top, low = refs[-4:]
     i, j = pl.program_id(0), pl.program_id(1)
     height = own.shape[1]
@@ -218,15 +219,15 @@
 
     @pl.when(j == 0)
     def _():
-        out[...] = start[...]
+        out[...] = sum((start[...] for start in starts), jnp.zeros_like(out))
 
     a_top, a_low = split(c[0])
     out[...] -= mm3(a_top, a_low, top[j], low[j])
 
 
-def finish(idx, first, own, other, blocks, start, solved):
+def finish(idx, first, own, other, blocks, starts, solved):
     n, height, columns = own.shape
-    rows = start.shape[0]
+    rows = blocks.shape[1]
     pair = 2 * height
     tile = rows // 2
     hbm = pl.BlockSpec(memory_space=pltpu.HBM)
@@ -238,26 +239,26 @@
     part = pl.BlockSpec((tile, columns), lambda i, j: (i, 0))
     term = pltpu.VMEM((n, pair, columns), jnp.bfloat16)
     return pl.pallas_call(
-        finish_kernel,
+        functools.partial(finish_kernel, len(starts)),
         grid=(rows // tile, n),
-        out_shape=[jax.ShapeDtypeStruct((NX * pair, columns), jnp.float32), jax.ShapeDtypeStruct(start.shape, jnp.float32)],
+        out_shape=[jax.ShapeDtypeStruct((NX * pair, columns), jnp.float32), jax.ShapeDtypeStruct((rows, columns), jnp.float32)],
         in_specs=[
             pl.BlockSpec(memory_space=pltpu.SMEM),
             block,
             block,
             pl.BlockSpec((1, tile, pair), lambda i, j: (first + j, i, 0)),
-            part,
         ]
+        + [part] * len(starts)
         + [hbm] * len(solved),
         out_specs=[pl.BlockSpec((pair, columns), lambda i, j: (first + once(i, j), 0)), part],
         scratch_shapes=[term, term],
-        input_output_aliases={5: 0} if solved else {},
-        compiler_params=pltpu.CompilerParams(vmem_limit_bytes=40 * MIB),
+        input_output_aliases={4 + len(starts): 0} if solved else {},
+        compiler_params=pltpu.CompilerParams(vmem_limit_bytes=34 * MIB),
         cost_estimate=pl.CostEstimate(
             flops=6 * n * rows * pair * columns, bytes_accessed=n * 8 * MIB, transcendentals=0
         ),
         name="finish_pairs",
-    )(idx, own, other, blocks, start, *solved)
+    )(idx, own, other, blocks, *starts, *solved)
 
 
 def hand_kernel(first, idx, filled, begin, end, taken, own, other, *refs):
@@ -311,7 +312,7 @@
         out_specs=slab,
         scratch_shapes=[pltpu.VMEM((n * 2 * height, columns), jnp.float32), pltpu.SemaphoreType.DMA((2 * n,))],
         input_output_aliases={7: 0} if before else {},
-        compiler_params=pltpu.CompilerParams(vmem_limit_bytes=32 * MIB),
+        compiler_params=pltpu.CompilerParams(vmem_limit_bytes=16 * MIB),
         cost_estimate=pl.CostEstimate(flops=0, bytes_accessed=n * 4 * MIB, transcendentals=0),
         name="hand_down",
     )(idx, filled, begin, end, taken, own, other, *before)
@@ -379,12 +380,13 @@
     handed = hand(2, idx, filled, begin, jnp.full_like(begin, rows_taken.shape[1]), rows_taken, early, early_other, ())
 
     early, early_other, handed = lax.optimization_barrier((early, early_other, handed))
-    solved, remaining = finish(idx, 2, early, early_other, gathered, rhs_head, ())
+    solved, remaining = finish(idx, 2, early, early_other, gathered, (), ())
     last_pieces, remaining = lax.optimization_barrier((last_pieces, remaining))
+    last_other = [both_cores(piece) for piece in (last, *last_pieces)]
     last = join(idx, (last, *last_pieces))
-    last_other = both_cores(last)
+    last_other = join(idx, last_other)
     handed = hand(0, idx, filled, jnp.zeros_like(begin), begin, rows_taken, last, last_other, (handed,))
-    solved, remaining = finish(idx, 0, last, last_other, gathered, remaining, (solved,))
+    solved, remaining = finish(idx, 0, last, last_other, gathered, (rhs_head, remaining), (solved,))
     return (remaining, solved, handed)
 
 

time: 211 us -> 209 us (level)
  waiting for transfers between devices: 51.2 us -> 48.9 us
    ppermute x9 -> x12, waiting for transfers between devices: 9.65 us -> 6.56 us  [both_cores(): return lax.ppermute(own, 'core', SWAP)]
    ppermute x9 -> x12, starting transfers between devices: 9.72 us -> 11.2 us  [both_cores(): return lax.ppermute(own, 'core', SWAP)]
    pallas_call x2 -> x3, Pallas kernels: 3.72 us -> 4.69 us  [join(): pl.pallas_call(functools.partial(join_kernel, tuple((len(group) for group...]
  transfers between devices with their start and end apart: 41 -> 44, of which waited for: 17 -> 18; matrix products, arithmetic and copies ran while one was open for 7% -> 7% of each run, Pallas kernels for 16% -> 17%
where the time goes in v2:
time: 209 us; the launch traced here: 208 us
  Pallas kernels  53.4 us (26%)
  waiting for transfers between devices  48.9 us (23%)
  starting transfers between devices  41.3 us (20%)
  blocking collectives  33.2 us (16%)
  between operations  14.6 us (7%)
  local copies, waits for them, and re-layouts  11.6 us (6%)
  other arithmetic  5.31 us (3%)
    all_to_all x1, blocking collectives, on_device(): lax.all_to_all(packed, 'y', split_axis=0, concat_axis=0, tiled=True)  33.2 us
    pallas_call x2, Pallas kernels, finish(): pl.pallas_call(functools.partial(finish_kernel, len(starts)), grid=(rows...  22.3 us
    ppermute x12, waiting for transfers between devices, on_device(): got = [lax.ppermute(mine, 'x', [(p, (p + s) % NX)]) for s in (2, 3, 1)]  20 us
    ppermute x12, starting transfers between devices, on_device(): got = [lax.ppermute(mine, 'x', [(p, (p + s) % NX)]) for s in (2, 3, 1)]  15.3 us
    ppermute x8, waiting for transfers between devices, neighbours_y(): return (lax.ppermute(piece, 'y', ONE), lax.ppermute(piece, 'y', THREE))  14.1 us
    pallas_call x2, Pallas kernels, hand(): pl.pallas_call(functools.partial(hand_kernel, first), grid=(slots,), out_...  11.3 us
    ppermute x12, starting transfers between devices, both_cores(): return lax.ppermute(own, 'core', SWAP)  11.2 us
    pallas_call x3, Pallas kernels, update(): pl.pallas_call(functools.partial(update_kernel, p), out_shape=jax.ShapeDt...  9.37 us
  transfers between devices with their start and end apart: 44, of which 18 were waited for; matrix products, arithmetic and copies ran while one was open for 7% of the time, Pallas kernels for 17%

profile of v2, /device:TPU:1, one launch (start us, length us, event | category | flops | bytes accessed | tf_op | source)
XLA Modules:
  0.0 208.2 jit_solution(75835171417387455)
XLA Ops:
  9.9 33.2 %all_to_all.5.fac_own = f32[4,128,1152]{2,1,0:T(8,128)S(1)} all-to-all(f32[4,128,1152]{2,1,0:T(8,128)S(1)} %pad_maximum_fusion), channel_id=1, replica_groups=mesh['x'=4,'y'=4,'core'=2,'z'=4] {'y'}, dimensions={0} | all-to-all | bytes 4718592 | tf_op jit(solution)/shard_map/all_to_all | solution.py:339
  43.1 1.9 collective-permute-start
  44.9 1.2 fusion.5
  47.1 2.1 %collective-permute-done.fac_other = f32[4,128,1152]{2,1,0:T(8,128)} collective-permute-done((f32[4,128,1152]{2,1,0:T(8,128)S(1)}, f32[4,128,1152]{2,1,0:T(8,128)}, u32[]{:S(2)}, u32[]{:S(2)}) %collective-permute-start) | collective-permute-done | bytes 2359328 | tf_op jit(solution)/shard_map/ppermute | solution.py:53
  50.8 1.4 collective-permute-start.1
  52.2 1.4 collective-permute-start.2
  53.5 1.3 collective-permute-start.3
  54.8 6.4 %collective-permute-done.6.far = f32[128,1024]{1,0:T(8,128)S(1)} collective-permute-done((f32[128,1024]{1,0:T(8,128)}, f32[128,1024]{1,0:T(8,128)S(1)}, u32[]{:S(2)}, u32[]{:S(2)}) %collective-permute-start.6) | collective-permute-done | bytes 524320 | tf_op jit(solution)/shard_map/ppermute | solution.py:60
  63.4 4.9 %collective-permute-done.3 = f32[512,128]{1,0:T(8,128)} collective-permute-done((f32[512,128]{1,0:T(8,128)S(1)}, f32[512,128]{1,0:T(8,128)}, u32[]{:S(2)}, u32[]{:S(2)}) %collective-permute-start.3) | collective-permute-done | bytes 262176 | tf_op jit(solution)/shard_map/ppermute | solution.py:354
  68.3 1.2 add_select_fusion.2.mine
  72.7 2.9 %update_rows.3.r_own = f32[4,128,128]{2,1,0:T(8,128)S(1)} custom-call(s32[4]{0:T(128)S(1)} %pad_add_fusion.idx, f32[512,128]{1,0:T(8,128)S(1)} %add_select_fusion.2.mine, f32[512,128]{1,0:T(8,128)S(1)} %collective-permute-done.4.other, f32[4,128,128]{2,1,0:T(8,128)S(1)} %slice.52.r_own, f32[128,4096]{1,0:T(8,128)S(1)} %copy-done.1, ...), custom_call_target="tpu_custom_call" | custom-call | flops 1000 | bytes 1000 | tf_op jit(solution)/shard_map/update_rows/pallas_call | solution.py:155
  76.5 1.2 collective-permute-done.9.r_other
  78.2 1.3 collective-permute-start.10
  80.2 1.4 collective-permute-start.12
  81.6 3.9 %collective-permute-done.15.far = f32[128,1024]{1,0:T(8,128)} collective-permute-done((f32[128,1024]{1,0:T(8,128)}, f32[128,1024]{1,0:T(8,128)}, u32[]{:S(2)}, u32[]{:S(2)}) %collective-permute-start.15) | collective-permute-done | bytes 524320 | tf_op jit(solution)/shard_map/ppermute | solution.py:60
  88.5 3.6 %collective-permute-done.10 = f32[512,128]{1,0:T(8,128)} collective-permute-done((f32[512,128]{1,0:T(8,128)S(1)}, f32[512,128]{1,0:T(8,128)}, u32[]{:S(2)}, u32[]{:S(2)}) %collective-permute-start.10) | collective-permute-done | bytes 262176 | tf_op jit(solution)/shard_map/ppermute | solution.py:354
  92.8 1.2 add_select_fusion.1.mine
  93.9 1.4 collective-permute-start.13
  95.4 1.3 collective-permute-start.28
  97.8 3.3 %update_rows.4.r_own = f32[4,128,128]{2,1,0:T(8,128)S(1)} custom-call(s32[4]{0:T(128)S(1)} %pad_add_fusion.idx, f32[512,128]{1,0:T(8,128)S(1)} %add_select_fusion.1.mine, f32[512,128]{1,0:T(8,128)S(1)} %collective-permute-done.13.other, f32[4,128,128]{2,1,0:T(8,128)S(1)} %update_rows.3.r_own, f32[128,4096]{1,0:T(8,128)S(1)} %copy-done.2, ...), custom_call_target="tpu_custom_call" | custom-call | flops 1000 | bytes 1000 | tf_op jit(solution)/shard_map/update_rows/pallas_call | solution.py:155
  101.8 1.2 collective-permute-done.22.r_other
  103.6 1.4 collective-permute-start.23
  105.0 1.3 collective-permute-start.24
  106.3 1.4 collective-permute-start.25
  107.6 2.8 %collective-permute-done.28.far = f32[128,1024]{1,0:T(8,128)} collective-permute-done((f32[128,1024]{1,0:T(8,128)}, f32[128,1024]{1,0:T(8,128)}, u32[]{:S(2)}, u32[]{:S(2)}) %collective-permute-start.28) | collective-permute-done | bytes 524320 | tf_op jit(solution)/shard_map/ppermute | solution.py:60
  112.4 1.8 collective-permute-start.30
  114.3 7.1 %collective-permute-done.24 = f32[512,128]{1,0:T(8,128)} collective-permute-done((f32[512,128]{1,0:T(8,128)S(1)}, f32[512,128]{1,0:T(8,128)}, u32[]{:S(2)}, u32[]{:S(2)}) %collective-permute-start.24) | collective-permute-done | bytes 262176 | tf_op jit(solution)/shard_map/ppermute | solution.py:354
  121.4 1.2 add_select_fusion.mine
  125.5 3.1 %update_rows.5.r_own = f32[4,128,128]{2,1,0:T(8,128)S(1)} custom-call(s32[4]{0:T(128)S(1)} %pad_add_fusion.idx, f32[512,128]{1,0:T(8,128)S(1)} %add_select_fusion.mine, f32[512,128]{1,0:T(8,128)S(1)} %collective-permute-done.26.other, f32[4,128,128]{2,1,0:T(8,128)S(1)} %update_rows.4.r_own, f32[128,4096]{1,0:T(8,128)S(1)} %copy-done.3, ...), custom_call_target="tpu_custom_call" | custom-call | flops 1000 | bytes 1000 | tf_op jit(solution)/shard_map/update_rows/pallas_call | solution.py:155
  129.3 1.2 collective-permute-done.31.r_other
  130.5 3.9 %solve_pair.7 = f32[512,128]{1,0:T(8,128)S(1)} custom-call(s32[4]{0:T(128)S(1)} %pad_add_fusion.idx, f32[4,128,1152]{2,1,0:T(8,128)S(1)} %all_to_all.5.fac_own, f32[4,128,1152]{2,1,0:T(8,128)} %collective-permute-done.fac_other, f32[4,128,128]{2,1,0:T(8,128)S(1)} %update_rows.5.r_own, f32[4,128,128]{2,1,0:T(8,128)S(1)} %collective-permute-done.31.r_other), custom_call_target="tpu_custom_call" | custom-call | flops 1000 | bytes 1000 | tf_op jit(solution)/shard_map/solve_pair/pallas_call | solution.py:109
  134.4 1.3 collective-permute-start.32
  135.7 1.3 collective-permute-start.33
  137.0 1.3 collective-permute-start.34
  140.6 1.9 collective-permute-start.21
  142.6 4.3 %collective-permute-done.34 = f32[512,128]{1,0:T(8,128)S(1)} collective-permute-done((f32[512,128]{1,0:T(8,128)S(1)}, f32[512,128]{1,0:T(8,128)S(1)}, u32[]{:S(2)}, u32[]{:S(2)}) %collective-permute-start.34) | collective-permute-done | bytes 262176 | tf_op jit(solution)/shard_map/ppermute | solution.py:354
  147.0 2.2 %collective-permute-done.21.refs_4_ = f32[2,256,128]{2,1,0:T(8,128)S(1)} collective-permute-done((f32[2,256,128]{2,1,0:T(8,128)S(1)}, f32[2,256,128]{2,1,0:T(8,128)S(1)}, u32[]{:S(2)}, u32[]{:S(2)}) %collective-permute-start.21) | collective-permute-done | bytes 262176 | tf_op jit(solution)/shard_map/ppermute | solution.py:66
  149.2 1.8 join_columns.3.own
  151.0 1.5 collective-permute-start.38
  153.4 1.8 collective-permute-start.36
  155.2 1.4 collective-permute-start.37
  157.4 5.8 %hand_down.2.refs_0_ = f32[4,256,512]{2,1,0:T(8,128)} custom-call(s32[4]{0:T(128)S(1)} %pad_add_fusion.idx, s32[4]{0:T(128)S(1)} %convert_element_type.10.filled, s32[4]{0:T(128)S(1)} %convert_reduce_fusion.begin.end, s32[4]{0:T(128)S(1)} %broadcast_3_end.2.end, s32[4,256]{1,0:T(4,128)S(1)} %select_reduce_fusion.taken, f32[2,512,512]{2,1,0:T(8,128)S(1)} %join_columns.3.own, ...), custom_call_target="tpu_custom_call" | custom-call | bytes 8388608 | tf_op jit(solution)/shard_map/hand_down/pallas_call | solution.py:307
  163.2 3.8 %all-gather.3.cloned.1.call-done = f32[4096,1024]{1,0:T(8,128)} async-done(((f32[1024,1024]{1,0:T(8,128)}), f32[4096,1024]{1,0:T(8,128)}) %all-gather.3.cloned.1.call-update) | async-done | bytes 16777232 | tf_op jit(solution)/shard_map/all_gather | solution.py:333
  167.1 11.1 %finish_pairs.2 = (f32[4096,512]{1,0:T(8,128)}, f32[1024,512]{1,0:T(8,128)S(1)}) custom-call(s32[4]{0:T(128)S(1)} %pad_add_fusion.idx, f32[2,512,512]{2,1,0:T(8,128)S(1)} %join_columns.3.own, f32[2,512,512]{2,1,0:T(8,128)} %collective-permute-done.38.other, f32[4,1024,1024]{2,1,0:T(8,128)} %bitcast.17), custom_call_target="tpu_custom_call" | custom-call | flops 6442450944 | bytes 16777216 | tf_op jit(solution)/shard_map/finish_pairs/pallas_call | solution.py:241
  178.2 1.5 collective-permute-done.37.refs_3_
  181.0 2.0 join_columns.4.own
  184.7 5.5 %hand_down.3 = f32[4,256,512]{2,1,0:T(8,128)} custom-call(s32[4]{0:T(128)S(1)} %pad_add_fusion.idx, s32[4]{0:T(128)S(1)} %convert_element_type.10.filled, s32[4]{0:T(128)S(1)} %broadcast_2_begin.2.begin, s32[4]{0:T(128)S(1)} %convert_reduce_fusion.begin.end, s32[4,256]{1,0:T(4,128)S(1)} %select_reduce_fusion.taken, ...), custom_call_target="tpu_custom_call", output_to_operand_aliasing={{}: (7, {})} | custom-call | bytes 8388608 | tf_op jit(solution)/shard_map/hand_down/pallas_call | solution.py:307
  190.2 11.2 %finish_pairs.3 = (f32[4096,512]{1,0:T(8,128)}, f32[1024,512]{1,0:T(8,128)}) custom-call(s32[4]{0:T(128)S(1)} %pad_add_fusion.idx, f32[2,512,512]{2,1,0:T(8,128)S(1)} %join_columns.4.own, f32[2,512,512]{2,1,0:T(8,128)S(1)} %join_columns.5.other, f32[4,1024,1024]{2,1,0:T(8,128)} %bitcast.18, ...), custom_call_target="tpu_custom_call", output_to_operand_aliasing={{0}: (6, {})} | custom-call | flops 6442450944 | bytes 16777216 | tf_op jit(solution)/shard_map/finish_pairs/pallas_call | solution.py:241
  (117 shorter events, 31.6 us)
Async XLA Ops:
  7.2 159.9 %all-gather.3.cloned.1.call-start = ((), (), s32[]{:S(2)}) async-start(), calls=%async_computation.1 | async-start | bytes 20971520 | tf_op jit(solution)/shard_map/all_gather | solution.py:333
  9.9 35.1 %copy-start = (f32[128,4096]{1,0:T(8,128)S(1)}, f32[128,4096]{1,0:T(8,128)}, u32[]{:S(2)}) copy-start(f32[128,4096]{1,0:T(8,128)} %trailing.5) | copy-start | bytes 6291460
  43.1 6.2 %collective-permute-start = (f32[4,128,1152]{2,1,0:T(8,128)S(1)}, f32[4,128,1152]{2,1,0:T(8,128)}, u32[]{:S(2)}, u32[]{:S(2)}) collective-permute-start(f32[4,128,1152]{2,1,0:T(8,128)S(1)} %all_to_all.5.fac_own), channel_id=1, source_target_pairs={{0,4},{4,0},{1,5},{5,1},{2,6},{6,2},{3,7},{7,3},{8,12},{12,8},{9,1... | collective-permute-start | bytes 7077896 | tf_op jit(solution)/shard_map/ppermute | solution.py:53
  46.1 15.1 %collective-permute-start.6 = (f32[128,1024]{1,0:T(8,128)}, f32[128,1024]{1,0:T(8,128)S(1)}, u32[]{:S(2)}, u32[]{:S(2)}) collective-permute-start(f32[128,1024]{1,0:T(8,128)} %get-tuple-element.24), channel_id=1, source_target_pairs={{0,24},{8,16},{16,8},{24,0},{1,25},{9,17},{17,9},{25,1},{2,26},{10... | collective-permute-start | bytes 1572872 | tf_op jit(solution)/shard_map/ppermute | solution.py:60
  47.0 14.3 %collective-permute-start.5 = (f32[128,1024]{1,0:T(8,128)}, f32[128,1024]{1,0:T(8,128)}, u32[]{:S(2)}, u32[]{:S(2)}) collective-permute-start(f32[128,1024]{1,0:T(8,128)} %get-tuple-element.24), channel_id=1, source_target_pairs={{0,8},{8,0},{16,24},{24,16},{1,9},{9,1},{17,25},{25,17},{2,10},{10... | collective-permute-start | bytes 1572872 | tf_op jit(solution)/shard_map/ppermute | solution.py:60
  50.8 12.6 %collective-permute-start.1 = (f32[512,128]{1,0:T(8,128)S(1)}, f32[512,128]{1,0:T(8,128)}, u32[]{:S(2)}, u32[]{:S(2)}) collective-permute-start(f32[512,128]{1,0:T(8,128)S(1)} %solve_pair.4), channel_id=1, source_target_pairs={{96,32},{97,33},{98,34},{99,35},{100,36},{101,37},{102,38},{103,39... | collective-permute-start | bytes 786440 | tf_op jit(solution)/shard_map/ppermute | solution.py:354
  52.2 11.2 %collective-permute-start.2 = (f32[512,128]{1,0:T(8,128)S(1)}, f32[512,128]{1,0:T(8,128)}, u32[]{:S(2)}, u32[]{:S(2)}) collective-permute-start(f32[512,128]{1,0:T(8,128)S(1)} %solve_pair.4), channel_id=1, source_target_pairs={{96,64},{97,65},{98,66},{99,67},{100,68},{101,69},{102,70},{103,71... | collective-permute-start | bytes 786440 | tf_op jit(solution)/shard_map/ppermute | solution.py:354
  53.5 14.8 %collective-permute-start.3 = (f32[512,128]{1,0:T(8,128)S(1)}, f32[512,128]{1,0:T(8,128)}, u32[]{:S(2)}, u32[]{:S(2)}) collective-permute-start(f32[512,128]{1,0:T(8,128)S(1)} %solve_pair.4), channel_id=1, source_target_pairs={{96,0},{97,1},{98,2},{99,3},{100,4},{101,5},{102,6},{103,7},{104,8... | collective-permute-start | bytes 786440 | tf_op jit(solution)/shard_map/ppermute | solution.py:354
  54.8 16.8 %copy-start.1 = (f32[128,4096]{1,0:T(8,128)S(1)}, f32[128,4096]{1,0:T(8,128)}, u32[]{:S(2)}) copy-start(f32[128,4096]{1,0:T(8,128)} %trailing.5) | copy-start | bytes 6291460
  61.2 10.2 %collective-permute-start.7 = (f32[64,1024]{1,0:T(8,128)S(1)}, f32[64,1024]{1,0:T(8,128)S(1)}, u32[]{:S(2)}, u32[]{:S(2)}) collective-permute-start(f32[64,1024]{1,0:T(8,128)S(1)} %slice.54), channel_id=1, source_target_pairs={{0,8},{8,0},{16,24},{24,16},{1,9},{9,1},{17,25},{25,17},{2,10},{10... | collective-permute-start | bytes 786440 | tf_op jit(solution)/shard_map/ppermute | solution.py:65
  62.4 9.0 %collective-permute-start.8 = (f32[64,1024]{1,0:T(8,128)S(1)}, f32[64,1024]{1,0:T(8,128)S(1)}, u32[]{:S(2)}, u32[]{:S(2)}) collective-permute-start(f32[64,1024]{1,0:T(8,128)S(1)} %slice.55), channel_id=1, source_target_pairs={{0,24},{8,16},{16,8},{24,0},{1,25},{9,17},{17,9},{25,1},{2,26},{10... | collective-permute-start | bytes 786440 | tf_op jit(solution)/shard_map/ppermute | solution.py:66
  69.5 2.1 %collective-permute-start.4 = (f32[512,128]{1,0:T(8,128)S(1)}, f32[512,128]{1,0:T(8,128)S(1)}, u32[]{:S(2)}, u32[]{:S(2)}) collective-permute-start(f32[512,128]{1,0:T(8,128)S(1)} %add_select_fusion.2.mine), channel_id=1, source_target_pairs={{0,4},{4,0},{1,5},{5,1},{2,6},{6,2},{3,7},{7,3},{8,12},{12,8},{9,1... | collective-permute-start | bytes 786440 | tf_op jit(solution)/shard_map/ppermute | solution.py:53
  70.5 15.0 %collective-permute-start.15 = (f32[128,1024]{1,0:T(8,128)}, f32[128,1024]{1,0:T(8,128)}, u32[]{:S(2)}, u32[]{:S(2)}) collective-permute-start(f32[128,1024]{1,0:T(8,128)} %get-tuple-element.25), channel_id=1, source_target_pairs={{0,24},{8,16},{16,8},{24,0},{1,25},{9,17},{17,9},{25,1},{2,26},{10... | collective-permute-start | bytes 1572872 | tf_op jit(solution)/shard_map/ppermute | solution.py:60
  71.4 15.2 %collective-permute-start.14 = (f32[128,1024]{1,0:T(8,128)}, f32[128,1024]{1,0:T(8,128)}, u32[]{:S(2)}, u32[]{:S(2)}) collective-permute-start(f32[128,1024]{1,0:T(8,128)} %get-tuple-element.25), channel_id=1, source_target_pairs={{0,8},{8,0},{16,24},{24,16},{1,9},{9,1},{17,25},{25,17},{2,10},{10... | collective-permute-start | bytes 1572872 | tf_op jit(solution)/shard_map/ppermute | solution.py:60
  75.6 2.0 collective-permute-start.9
  78.2 13.8 %collective-permute-start.10 = (f32[512,128]{1,0:T(8,128)S(1)}, f32[512,128]{1,0:T(8,128)}, u32[]{:S(2)}, u32[]{:S(2)}) collective-permute-start(f32[512,128]{1,0:T(8,128)S(1)} %solve_pair.5), channel_id=1, source_target_pairs={{64,0},{65,1},{66,2},{67,3},{68,4},{69,5},{70,6},{71,7},{72,8},{73... | collective-permute-start | bytes 786440 | tf_op jit(solution)/shard_map/ppermute | solution.py:354
  79.5 12.5 %collective-permute-start.11 = (f32[512,128]{1,0:T(8,128)S(1)}, f32[512,128]{1,0:T(8,128)S(1)}, u32[]{:S(2)}, u32[]{:S(2)}) collective-permute-start(f32[512,128]{1,0:T(8,128)S(1)} %solve_pair.5), channel_id=1, source_target_pairs={{64,32},{65,33},{66,34},{67,35},{68,36},{69,37},{70,38},{71,39},{7... | collective-permute-start | bytes 786440 | tf_op jit(solution)/shard_map/ppermute | solution.py:354
  80.2 12.5 %collective-permute-start.12 = (f32[512,128]{1,0:T(8,128)S(1)}, f32[512,128]{1,0:T(8,128)}, u32[]{:S(2)}, u32[]{:S(2)}) collective-permute-start(f32[512,128]{1,0:T(8,128)S(1)} %solve_pair.5), channel_id=1, source_target_pairs={{64,96},{65,97},{66,98},{67,99},{68,100},{69,101},{70,102},{71,103... | collective-permute-start | bytes 786440 | tf_op jit(solution)/shard_map/ppermute | solution.py:354
  86.4 11.3 %collective-permute-start.16 = (f32[64,1024]{1,0:T(8,128)S(1)}, f32[64,1024]{1,0:T(8,128)S(1)}, u32[]{:S(2)}, u32[]{:S(2)}) collective-permute-start(f32[64,1024]{1,0:T(8,128)S(1)} %slice.56), channel_id=1, source_target_pairs={{0,8},{8,0},{16,24},{24,16},{1,9},{9,1},{17,25},{25,17},{2,10},{10... | collective-permute-start | bytes 786440 | tf_op jit(solution)/shard_map/ppermute | solution.py:65
  87.5 10.3 %collective-permute-start.17 = (f32[64,1024]{1,0:T(8,128)S(1)}, f32[64,1024]{1,0:T(8,128)S(1)}, u32[]{:S(2)}, u32[]{:S(2)}) collective-permute-start(f32[64,1024]{1,0:T(8,128)S(1)} %slice.57), channel_id=1, source_target_pairs={{0,24},{8,16},{16,8},{24,0},{1,25},{9,17},{17,9},{25,1},{2,26},{10... | collective-permute-start | bytes 786440 | tf_op jit(solution)/shard_map/ppermute | solution.py:66
  93.9 3.9 %collective-permute-start.13 = (f32[512,128]{1,0:T(8,128)S(1)}, f32[512,128]{1,0:T(8,128)S(1)}, u32[]{:S(2)}, u32[]{:S(2)}) collective-permute-start(f32[512,128]{1,0:T(8,128)S(1)} %add_select_fusion.1.mine), channel_id=1, source_target_pairs={{0,4},{4,0},{1,5},{5,1},{2,6},{6,2},{3,7},{7,3},{8,12},{12,8},{9,1... | collective-permute-start | bytes 786440 | tf_op jit(solution)/shard_map/ppermute | solution.py:53
  95.4 15.0 %collective-permute-start.28 = (f32[128,1024]{1,0:T(8,128)}, f32[128,1024]{1,0:T(8,128)}, u32[]{:S(2)}, u32[]{:S(2)}) collective-permute-start(f32[128,1024]{1,0:T(8,128)} %get-tuple-element.28), channel_id=1, source_target_pairs={{0,24},{8,16},{16,8},{24,0},{1,25},{9,17},{17,9},{25,1},{2,26},{10... | collective-permute-start | bytes 1572872 | tf_op jit(solution)/shard_map/ppermute | solution.py:60
  96.7 14.8 %collective-permute-start.27 = (f32[128,1024]{1,0:T(8,128)}, f32[128,1024]{1,0:T(8,128)}, u32[]{:S(2)}, u32[]{:S(2)}) collective-permute-start(f32[128,1024]{1,0:T(8,128)} %get-tuple-element.28), channel_id=1, source_target_pairs={{0,8},{8,0},{16,24},{24,16},{1,9},{9,1},{17,25},{25,17},{2,10},{10... | collective-permute-start | bytes 1572872 | tf_op jit(solution)/shard_map/ppermute | solution.py:60
  101.1 1.9 collective-permute-start.22
  103.6 17.8 %copy-start.7 = (f32[512,128]{1,0:T(8,128)}, f32[512,128]{1,0:T(8,128)S(1)}, u32[]{:S(2)}) copy-start(f32[512,128]{1,0:T(8,128)S(1)} %solve_pair.6) | copy-start | bytes 786436
  103.6 10.7 %collective-permute-start.23 = (f32[512,128]{1,0:T(8,128)S(1)}, f32[512,128]{1,0:T(8,128)}, u32[]{:S(2)}, u32[]{:S(2)}) collective-permute-start(f32[512,128]{1,0:T(8,128)S(1)} %solve_pair.6), channel_id=1, source_target_pairs={{32,96},{33,97},{34,98},{35,99},{36,100},{37,101},{38,102},{39,103... | collective-permute-start | bytes 786440 | tf_op jit(solution)/shard_map/ppermute | solution.py:354
  105.0 16.4 %collective-permute-start.24 = (f32[512,128]{1,0:T(8,128)S(1)}, f32[512,128]{1,0:T(8,128)}, u32[]{:S(2)}, u32[]{:S(2)}) collective-permute-start(f32[512,128]{1,0:T(8,128)S(1)} %solve_pair.6), channel_id=1, source_target_pairs={{32,0},{33,1},{34,2},{35,3},{36,4},{37,5},{38,6},{39,7},{40,8},{41... | collective-permute-start | bytes 786440 | tf_op jit(solution)/shard_map/ppermute | solution.py:354
  106.3 15.1 %collective-permute-start.25 = (f32[512,128]{1,0:T(8,128)S(1)}, f32[512,128]{1,0:T(8,128)}, u32[]{:S(2)}, u32[]{:S(2)}) collective-permute-start(f32[512,128]{1,0:T(8,128)S(1)} %solve_pair.6), channel_id=1, source_target_pairs={{32,64},{33,65},{34,66},{35,67},{36,68},{37,69},{38,70},{39,71},{4... | collective-permute-start | bytes 786440 | tf_op jit(solution)/shard_map/ppermute | solution.py:354
  107.6 17.9 %copy-start.3 = (f32[128,4096]{1,0:T(8,128)S(1)}, f32[128,4096]{1,0:T(8,128)}, u32[]{:S(2)}) copy-start(f32[128,4096]{1,0:T(8,128)} %trailing.5) | copy-start | bytes 6291460
  111.4 14.1 %collective-permute-start.29 = (f32[64,1024]{1,0:T(8,128)S(1)}, f32[64,1024]{1,0:T(8,128)S(1)}, u32[]{:S(2)}, u32[]{:S(2)}) collective-permute-start(f32[64,1024]{1,0:T(8,128)S(1)} %slice.60), channel_id=1, source_target_pairs={{0,8},{8,0},{16,24},{24,16},{1,9},{9,1},{17,25},{25,17},{2,10},{10... | collective-permute-start | bytes 786440 | tf_op jit(solution)/shard_map/ppermute | solution.py:65
  112.4 13.0 %collective-permute-start.30 = (f32[64,1024]{1,0:T(8,128)S(1)}, f32[64,1024]{1,0:T(8,128)S(1)}, u32[]{:S(2)}, u32[]{:S(2)}) collective-permute-start(f32[64,1024]{1,0:T(8,128)S(1)} %slice.61), channel_id=1, source_target_pairs={{0,24},{8,16},{16,8},{24,0},{1,25},{9,17},{17,9},{25,1},{2,26},{10... | collective-permute-start | bytes 786440 | tf_op jit(solution)/shard_map/ppermute | solution.py:66
  122.5 2.9 %collective-permute-start.26 = (f32[512,128]{1,0:T(8,128)S(1)}, f32[512,128]{1,0:T(8,128)S(1)}, u32[]{:S(2)}, u32[]{:S(2)}) collective-permute-start(f32[512,128]{1,0:T(8,128)S(1)} %add_select_fusion.mine), channel_id=1, source_target_pairs={{0,4},{4,0},{1,5},{5,1},{2,6},{6,2},{3,7},{7,3},{8,12},{12,8},{9,1... | collective-permute-start | bytes 786440 | tf_op jit(solution)/shard_map/ppermute | solution.py:53
  124.3 15.1 %collective-permute-start.19 = (f32[2,512,128]{2,1,0:T(8,128)}, f32[2,512,128]{2,1,0:T(8,128)S(1)}, u32[]{:S(2)}, u32[]{:S(2)}) collective-permute-start(f32[2,512,128]{2,1,0:T(8,128)} %pad_maximum_fusion.2.refs_0_), channel_id=1, source_target_pairs={{0,24},{8,16},{16,8},{24,0},{1,25},{9,17},{17,9},{25,1},{2,26},{10... | collective-permute-start | bytes 1572872 | tf_op jit(solution)/shard_map/ppermute | solution.py:60
  125.2 14.4 %collective-permute-start.18 = (f32[2,512,128]{2,1,0:T(8,128)}, f32[2,512,128]{2,1,0:T(8,128)}, u32[]{:S(2)}, u32[]{:S(2)}) collective-permute-start(f32[2,512,128]{2,1,0:T(8,128)} %pad_maximum_fusion.2.refs_0_), channel_id=1, source_target_pairs={{0,8},{8,0},{16,24},{24,16},{1,9},{9,1},{17,25},{25,17},{2,10},{10... | collective-permute-start | bytes 1572872 | tf_op jit(solution)/shard_map/ppermute | solution.py:60
  128.6 1.8 collective-permute-start.31
  134.4 8.1 %collective-permute-start.32 = (f32[512,128]{1,0:T(8,128)S(1)}, f32[512,128]{1,0:T(8,128)S(1)}, u32[]{:S(2)}, u32[]{:S(2)}) collective-permute-start(f32[512,128]{1,0:T(8,128)S(1)} %solve_pair.7), channel_id=1, source_target_pairs={{0,64},{1,65},{2,66},{3,67},{4,68},{5,69},{6,70},{7,71},{8,72},{9,... | collective-permute-start | bytes 786440 | tf_op jit(solution)/shard_map/ppermute | solution.py:354
  135.7 6.9 %collective-permute-start.33 = (f32[512,128]{1,0:T(8,128)S(1)}, f32[512,128]{1,0:T(8,128)S(1)}, u32[]{:S(2)}, u32[]{:S(2)}) collective-permute-start(f32[512,128]{1,0:T(8,128)S(1)} %solve_pair.7), channel_id=1, source_target_pairs={{0,96},{1,97},{2,98},{3,99},{4,100},{5,101},{6,102},{7,103},{8,104... | collective-permute-start | bytes 786440 | tf_op jit(solution)/shard_map/ppermute | solution.py:354
  137.0 9.9 %collective-permute-start.34 = (f32[512,128]{1,0:T(8,128)S(1)}, f32[512,128]{1,0:T(8,128)S(1)}, u32[]{:S(2)}, u32[]{:S(2)}) collective-permute-start(f32[512,128]{1,0:T(8,128)S(1)} %solve_pair.7), channel_id=1, source_target_pairs={{0,32},{1,33},{2,34},{3,35},{4,36},{5,37},{6,38},{7,39},{8,40},{9,... | collective-permute-start | bytes 786440 | tf_op jit(solution)/shard_map/ppermute | solution.py:354
  139.4 7.6 %collective-permute-start.20 = (f32[2,256,128]{2,1,0:T(8,128)S(1)}, f32[2,256,128]{2,1,0:T(8,128)S(1)}, u32[]{:S(2)}, u32[]{:S(2)}) collective-permute-start(f32[2,256,128]{2,1,0:T(8,128)S(1)} %slice.58), channel_id=1, source_target_pairs={{0,8},{8,0},{16,24},{24,16},{1,9},{9,1},{17,25},{25,17},{2,10},{10... | collective-permute-start | bytes 786440 | tf_op jit(solution)/shard_map/ppermute | solution.py:65
  140.6 8.6 %collective-permute-start.21 = (f32[2,256,128]{2,1,0:T(8,128)S(1)}, f32[2,256,128]{2,1,0:T(8,128)S(1)}, u32[]{:S(2)}, u32[]{:S(2)}) collective-permute-start(f32[2,256,128]{2,1,0:T(8,128)S(1)} %slice.59), channel_id=1, source_target_pairs={{0,24},{8,16},{16,8},{24,0},{1,25},{9,17},{17,9},{25,1},{2,26},{10... | collective-permute-start | bytes 786440 | tf_op jit(solution)/shard_map/ppermute | solution.py:66
  151.0 6.4 %collective-permute-start.38 = (f32[2,512,512]{2,1,0:T(8,128)S(1)}, f32[2,512,512]{2,1,0:T(8,128)}, u32[]{:S(2)}, u32[]{:S(2)}) collective-permute-start(f32[2,512,512]{2,1,0:T(8,128)S(1)} %join_columns.3.own), channel_id=1, source_target_pairs={{0,4},{4,0},{1,5},{5,1},{2,6},{6,2},{3,7},{7,3},{8,12},{12,8},{9,1... | collective-permute-start | bytes 6291464 | tf_op jit(solution)/shard_map/ppermute | solution.py:53
  153.2 24.9 %collective-permute-start.35 = (f32[2,512,128]{2,1,0:T(8,128)S(1)}, f32[2,512,128]{2,1,0:T(8,128)}, u32[]{:S(2)}, u32[]{:S(2)}) collective-permute-start(f32[2,512,128]{2,1,0:T(8,128)S(1)} %pad_maximum_fusion.3.refs_0_), channel_id=1, source_target_pairs={{0,8},{8,0},{16,24},{24,16},{1,9},{9,1},{17,25},{25,17},{2,10},{10... | collective-permute-start | bytes 1572872 | tf_op jit(solution)/shard_map/ppermute | solution.py:366
  153.4 24.7 %collective-permute-start.36 = (f32[2,512,128]{2,1,0:T(8,128)S(1)}, f32[2,512,128]{2,1,0:T(8,128)}, u32[]{:S(2)}, u32[]{:S(2)}) collective-permute-start(f32[2,512,128]{2,1,0:T(8,128)S(1)} %pad_maximum_fusion.3.refs_0_), channel_id=1, source_target_pairs={{0,24},{8,16},{16,8},{24,0},{1,25},{9,17},{17,9},{25,1},{2,26},{10... | collective-permute-start | bytes 1572872 | tf_op jit(solution)/shard_map/ppermute | solution.py:366
  155.2 24.5 %collective-permute-start.37 = (f32[2,512,128]{2,1,0:T(8,128)S(1)}, f32[2,512,128]{2,1,0:T(8,128)}, u32[]{:S(2)}, u32[]{:S(2)}) collective-permute-start(f32[2,512,128]{2,1,0:T(8,128)S(1)} %pad_maximum_fusion.3.refs_0_), channel_id=1, source_target_pairs={{0,16},{8,24},{16,0},{24,8},{1,17},{9,25},{17,1},{25,9},{2,18},{10... | collective-permute-start | bytes 1572872 | tf_op jit(solution)/shard_map/ppermute | solution.py:366
  156.5 26.5 %collective-permute-start.39 = (f32[2,512,128]{2,1,0:T(8,128)S(1)}, f32[2,512,128]{2,1,0:T(8,128)S(1)}, u32[]{:S(2)}, u32[]{:S(2)}) collective-permute-start(f32[2,512,128]{2,1,0:T(8,128)S(1)} %pad_maximum_fusion.3.refs_0_), channel_id=1, source_target_pairs={{0,4},{4,0},{1,5},{5,1},{2,6},{6,2},{3,7},{7,3},{8,12},{12,8},{9,1... | collective-permute-start | bytes 1572872 | tf_op jit(solution)/shard_map/ppermute | solution.py:53
  179.7 3.4 %collective-permute-start.40 = (f32[2,512,128]{2,1,0:T(8,128)}, f32[2,512,128]{2,1,0:T(8,128)S(1)}, u32[]{:S(2)}, u32[]{:S(2)}) collective-permute-start(f32[2,512,128]{2,1,0:T(8,128)} %collective-permute-done.35.refs_1_), channel_id=1, source_target_pairs={{0,4},{4,0},{1,5},{5,1},{2,6},{6,2},{3,7},{7,3},{8,12},{12,8},{9,1... | collective-permute-start | bytes 1572872 | tf_op jit(solution)/shard_map/ppermute | solution.py:53
  180.5 2.6 %collective-permute-start.41 = (f32[2,512,128]{2,1,0:T(8,128)}, f32[2,512,128]{2,1,0:T(8,128)S(1)}, u32[]{:S(2)}, u32[]{:S(2)}) collective-permute-start(f32[2,512,128]{2,1,0:T(8,128)} %collective-permute-done.36.refs_2_), channel_id=1, source_target_pairs={{0,4},{4,0},{1,5},{5,1},{2,6},{6,2},{3,7},{7,3},{8,12},{12,8},{9,1... | collective-permute-start | bytes 1572872 | tf_op jit(solution)/shard_map/ppermute | solution.py:53
  180.5 3.2 %collective-permute-start.42 = (f32[2,512,128]{2,1,0:T(8,128)}, f32[2,512,128]{2,1,0:T(8,128)S(1)}, u32[]{:S(2)}, u32[]{:S(2)}) collective-permute-start(f32[2,512,128]{2,1,0:T(8,128)} %collective-permute-done.37.refs_3_), channel_id=1, source_target_pairs={{0,4},{4,0},{1,5},{5,1},{2,6},{6,2},{3,7},{7,3},{8,12},{12,8},{9,1... | collective-permute-start | bytes 1572872 | tf_op jit(solution)/shard_map/ppermute | solution.py:53
  (9 other events, 40.3 us)
Sparse Core Ops, SparseCore 0:
  9.7 157.3 all-gather.2

commit v3 on v2

--- a/solution.py
+++ b/solution.py
@@ -288,14 +288,16 @@
             out[0, pl.ds(i, 1)] = rows[pl.ds(taken[slot, i] - first * 2 * height, 1)]
             return carry
 
-        def eight(m, carry):
-            for u in range(8):
-                one(begin[slot] + m * 8 + u, 0)
+        def sixteen(m, carry):
+            places = [begin[slot] + m * 16 + u for u in range(16)]
+            found = [rows[pl.ds(taken[slot, i] - first * 2 * height, 1)] for i in places]
+            for i, row in zip(places, found):
+                out[0, pl.ds(i, 1)] = row
             return carry
 
-        whole = lax.div(end[slot] - begin[slot], 8)
-        lax.fori_loop(0, whole, eight, 0)
-        lax.fori_loop(begin[slot] + whole * 8, end[slot], one, 0)
+        whole = lax.div(end[slot] - begin[slot], 16)
+        lax.fori_loop(0, whole, sixteen, 0)
+        lax.fori_loop(begin[slot] + whole * 16, end[slot], one, 0)
 
 
 def hand(first, idx, filled, begin, end, taken, own, other, before):

time: 209 us -> 209 us (level)
  no operation moved by 1% of the time
where the time goes in v3:
time: 209 us; the launch traced here: 208 us
  Pallas kernels  52.8 us (25%)
  waiting for transfers between devices  49 us (23%)
  starting transfers between devices  41.3 us (20%)
  blocking collectives  33.2 us (16%)
  between operations  14.6 us (7%)
  local copies, waits for them, and re-layouts  11.6 us (6%)
  other arithmetic  5.31 us (3%)
    all_to_all x1, blocking collectives, on_device(): lax.all_to_all(packed, 'y', split_axis=0, concat_axis=0, tiled=True)  33.2 us
    pallas_call x2, Pallas kernels, finish(): pl.pallas_call(functools.partial(finish_kernel, len(starts)), grid=(rows...  22.3 us
    ppermute x12, waiting for transfers between devices, on_device(): got = [lax.ppermute(mine, 'x', [(p, (p + s) % NX)]) for s in (2, 3, 1)]  20 us
    ppermute x12, starting transfers between devices, on_device(): got = [lax.ppermute(mine, 'x', [(p, (p + s) % NX)]) for s in (2, 3, 1)]  15.3 us
    ppermute x8, waiting for transfers between devices, neighbours_y(): return (lax.ppermute(piece, 'y', ONE), lax.ppermute(piece, 'y', THREE))  14.1 us
    ppermute x12, starting transfers between devices, both_cores(): return lax.ppermute(own, 'core', SWAP)  11.2 us
    pallas_call x2, Pallas kernels, hand(): pl.pallas_call(functools.partial(hand_kernel, first), grid=(slots,), out_...  10.8 us
    pallas_call x3, Pallas kernels, update(): pl.pallas_call(functools.partial(update_kernel, p), out_shape=jax.ShapeDt...  9.37 us
  transfers between devices with their start and end apart: 44, of which 18 were waited for; matrix products, arithmetic and copies ran while one was open for 7% of the time, Pallas kernels for 17%

profile of v3, /device:TPU:1, one launch (start us, length us, event | category | flops | bytes accessed | tf_op | source)
XLA Modules:
  0.0 207.9 jit_solution(1123150517856074977)
XLA Ops:
  9.9 33.2 %all_to_all.5.fac_own = f32[4,128,1152]{2,1,0:T(8,128)S(1)} all-to-all(f32[4,128,1152]{2,1,0:T(8,128)S(1)} %pad_maximum_fusion), channel_id=1, replica_groups=mesh['x'=4,'y'=4,'core'=2,'z'=4] {'y'}, dimensions={0} | all-to-all | bytes 4718592 | tf_op jit(solution)/shard_map/all_to_all | solution.py:341
  43.1 1.9 collective-permute-start
  44.9 1.2 fusion.5
  47.1 2.1 %collective-permute-done.fac_other = f32[4,128,1152]{2,1,0:T(8,128)} collective-permute-done((f32[4,128,1152]{2,1,0:T(8,128)S(1)}, f32[4,128,1152]{2,1,0:T(8,128)}, u32[]{:S(2)}, u32[]{:S(2)}) %collective-permute-start) | collective-permute-done | bytes 2359328 | tf_op jit(solution)/shard_map/ppermute | solution.py:53
  50.8 1.4 collective-permute-start.1
  52.2 1.4 collective-permute-start.2
  53.5 1.3 collective-permute-start.3
  54.8 6.4 %collective-permute-done.6.far = f32[128,1024]{1,0:T(8,128)S(1)} collective-permute-done((f32[128,1024]{1,0:T(8,128)}, f32[128,1024]{1,0:T(8,128)S(1)}, u32[]{:S(2)}, u32[]{:S(2)}) %collective-permute-start.6) | collective-permute-done | bytes 524320 | tf_op jit(solution)/shard_map/ppermute | solution.py:60
  63.4 4.9 %collective-permute-done.3 = f32[512,128]{1,0:T(8,128)} collective-permute-done((f32[512,128]{1,0:T(8,128)S(1)}, f32[512,128]{1,0:T(8,128)}, u32[]{:S(2)}, u32[]{:S(2)}) %collective-permute-start.3) | collective-permute-done | bytes 262176 | tf_op jit(solution)/shard_map/ppermute | solution.py:356
  68.3 1.2 add_select_fusion.2.mine
  72.7 2.9 %update_rows.3.r_own = f32[4,128,128]{2,1,0:T(8,128)S(1)} custom-call(s32[4]{0:T(128)S(1)} %pad_add_fusion.idx, f32[512,128]{1,0:T(8,128)S(1)} %add_select_fusion.2.mine, f32[512,128]{1,0:T(8,128)S(1)} %collective-permute-done.4.other, f32[4,128,128]{2,1,0:T(8,128)S(1)} %slice.52.r_own, f32[128,4096]{1,0:T(8,128)S(1)} %copy-done.1, ...), custom_call_target="tpu_custom_call" | custom-call | flops 1000 | bytes 1000 | tf_op jit(solution)/shard_map/update_rows/pallas_call | solution.py:155
  76.5 1.2 collective-permute-done.9.r_other
  78.2 1.3 collective-permute-start.10
  80.2 1.4 collective-permute-start.12
  81.6 3.9 %collective-permute-done.15.far = f32[128,1024]{1,0:T(8,128)} collective-permute-done((f32[128,1024]{1,0:T(8,128)}, f32[128,1024]{1,0:T(8,128)}, u32[]{:S(2)}, u32[]{:S(2)}) %collective-permute-start.15) | collective-permute-done | bytes 524320 | tf_op jit(solution)/shard_map/ppermute | solution.py:60
  88.5 3.6 %collective-permute-done.10 = f32[512,128]{1,0:T(8,128)} collective-permute-done((f32[512,128]{1,0:T(8,128)S(1)}, f32[512,128]{1,0:T(8,128)}, u32[]{:S(2)}, u32[]{:S(2)}) %collective-permute-start.10) | collective-permute-done | bytes 262176 | tf_op jit(solution)/shard_map/ppermute | solution.py:356
  92.8 1.2 add_select_fusion.1.mine
  93.9 1.4 collective-permute-start.13
  95.4 1.3 collective-permute-start.28
  97.8 3.3 %update_rows.4.r_own = f32[4,128,128]{2,1,0:T(8,128)S(1)} custom-call(s32[4]{0:T(128)S(1)} %pad_add_fusion.idx, f32[512,128]{1,0:T(8,128)S(1)} %add_select_fusion.1.mine, f32[512,128]{1,0:T(8,128)S(1)} %collective-permute-done.13.other, f32[4,128,128]{2,1,0:T(8,128)S(1)} %update_rows.3.r_own, f32[128,4096]{1,0:T(8,128)S(1)} %copy-done.2, ...), custom_call_target="tpu_custom_call" | custom-call | flops 1000 | bytes 1000 | tf_op jit(solution)/shard_map/update_rows/pallas_call | solution.py:155
  101.8 1.2 collective-permute-done.22.r_other
  103.6 1.4 collective-permute-start.23
  105.0 1.3 collective-permute-start.24
  106.3 1.4 collective-permute-start.25
  107.6 2.8 %collective-permute-done.28.far = f32[128,1024]{1,0:T(8,128)} collective-permute-done((f32[128,1024]{1,0:T(8,128)}, f32[128,1024]{1,0:T(8,128)}, u32[]{:S(2)}, u32[]{:S(2)}) %collective-permute-start.28) | collective-permute-done | bytes 524320 | tf_op jit(solution)/shard_map/ppermute | solution.py:60
  112.4 1.8 collective-permute-start.30
  114.3 7.1 %collective-permute-done.24 = f32[512,128]{1,0:T(8,128)} collective-permute-done((f32[512,128]{1,0:T(8,128)S(1)}, f32[512,128]{1,0:T(8,128)}, u32[]{:S(2)}, u32[]{:S(2)}) %collective-permute-start.24) | collective-permute-done | bytes 262176 | tf_op jit(solution)/shard_map/ppermute | solution.py:356
  121.4 1.2 add_select_fusion.mine
  125.5 3.1 %update_rows.5.r_own = f32[4,128,128]{2,1,0:T(8,128)S(1)} custom-call(s32[4]{0:T(128)S(1)} %pad_add_fusion.idx, f32[512,128]{1,0:T(8,128)S(1)} %add_select_fusion.mine, f32[512,128]{1,0:T(8,128)S(1)} %collective-permute-done.26.other, f32[4,128,128]{2,1,0:T(8,128)S(1)} %update_rows.4.r_own, f32[128,4096]{1,0:T(8,128)S(1)} %copy-done.3, ...), custom_call_target="tpu_custom_call" | custom-call | flops 1000 | bytes 1000 | tf_op jit(solution)/shard_map/update_rows/pallas_call | solution.py:155
  129.3 1.2 collective-permute-done.31.r_other
  130.5 3.9 %solve_pair.7 = f32[512,128]{1,0:T(8,128)S(1)} custom-call(s32[4]{0:T(128)S(1)} %pad_add_fusion.idx, f32[4,128,1152]{2,1,0:T(8,128)S(1)} %all_to_all.5.fac_own, f32[4,128,1152]{2,1,0:T(8,128)} %collective-permute-done.fac_other, f32[4,128,128]{2,1,0:T(8,128)S(1)} %update_rows.5.r_own, f32[4,128,128]{2,1,0:T(8,128)S(1)} %collective-permute-done.31.r_other), custom_call_target="tpu_custom_call" | custom-call | flops 1000 | bytes 1000 | tf_op jit(solution)/shard_map/solve_pair/pallas_call | solution.py:109
  134.4 1.3 collective-permute-start.32
  135.7 1.3 collective-permute-start.33
  137.0 1.3 collective-permute-start.34
  140.6 1.9 collective-permute-start.21
  142.6 4.3 %collective-permute-done.34 = f32[512,128]{1,0:T(8,128)S(1)} collective-permute-done((f32[512,128]{1,0:T(8,128)S(1)}, f32[512,128]{1,0:T(8,128)S(1)}, u32[]{:S(2)}, u32[]{:S(2)}) %collective-permute-start.34) | collective-permute-done | bytes 262176 | tf_op jit(solution)/shard_map/ppermute | solution.py:356
  147.0 2.2 %collective-permute-done.21.refs_4_ = f32[2,256,128]{2,1,0:T(8,128)S(1)} collective-permute-done((f32[2,256,128]{2,1,0:T(8,128)S(1)}, f32[2,256,128]{2,1,0:T(8,128)S(1)}, u32[]{:S(2)}, u32[]{:S(2)}) %collective-permute-start.21) | collective-permute-done | bytes 262176 | tf_op jit(solution)/shard_map/ppermute | solution.py:66
  149.2 1.8 join_columns.3.own
  151.0 1.5 collective-permute-start.38
  153.4 1.8 collective-permute-start.36
  155.2 1.4 collective-permute-start.37
  157.4 5.7 %hand_down.2.refs_0_ = f32[4,256,512]{2,1,0:T(8,128)} custom-call(s32[4]{0:T(128)S(1)} %pad_add_fusion.idx, s32[4]{0:T(128)S(1)} %convert_element_type.10.filled, s32[4]{0:T(128)S(1)} %convert_reduce_fusion.begin.end, s32[4]{0:T(128)S(1)} %broadcast_3_end.2.end, s32[4,256]{1,0:T(4,128)S(1)} %select_reduce_fusion.taken, f32[2,512,512]{2,1,0:T(8,128)S(1)} %join_columns.3.own, ...), custom_call_target="tpu_custom_call" | custom-call | bytes 8388608 | tf_op jit(solution)/shard_map/hand_down/pallas_call | solution.py:309
  163.1 4.0 %all-gather.3.cloned.1.call-done = f32[4096,1024]{1,0:T(8,128)} async-done(((f32[1024,1024]{1,0:T(8,128)}), f32[4096,1024]{1,0:T(8,128)}) %all-gather.3.cloned.1.call-update) | async-done | bytes 16777232 | tf_op jit(solution)/shard_map/all_gather | solution.py:335
  167.1 11.1 %finish_pairs.2 = (f32[4096,512]{1,0:T(8,128)}, f32[1024,512]{1,0:T(8,128)S(1)}) custom-call(s32[4]{0:T(128)S(1)} %pad_add_fusion.idx, f32[2,512,512]{2,1,0:T(8,128)S(1)} %join_columns.3.own, f32[2,512,512]{2,1,0:T(8,128)} %collective-permute-done.38.other, f32[4,1024,1024]{2,1,0:T(8,128)} %bitcast.17), custom_call_target="tpu_custom_call" | custom-call | flops 6442450944 | bytes 16777216 | tf_op jit(solution)/shard_map/finish_pairs/pallas_call | solution.py:241
  178.2 1.5 collective-permute-done.37.refs_3_
  181.0 2.0 join_columns.4.own
  184.7 5.1 %hand_down.3 = f32[4,256,512]{2,1,0:T(8,128)} custom-call(s32[4]{0:T(128)S(1)} %pad_add_fusion.idx, s32[4]{0:T(128)S(1)} %convert_element_type.10.filled, s32[4]{0:T(128)S(1)} %broadcast_2_begin.2.begin, s32[4]{0:T(128)S(1)} %convert_reduce_fusion.begin.end, s32[4,256]{1,0:T(4,128)S(1)} %select_reduce_fusion.taken, ...), custom_call_target="tpu_custom_call", output_to_operand_aliasing={{}: (7, {})} | custom-call | bytes 8388608 | tf_op jit(solution)/shard_map/hand_down/pallas_call | solution.py:309
  189.8 11.2 %finish_pairs.3 = (f32[4096,512]{1,0:T(8,128)}, f32[1024,512]{1,0:T(8,128)}) custom-call(s32[4]{0:T(128)S(1)} %pad_add_fusion.idx, f32[2,512,512]{2,1,0:T(8,128)S(1)} %join_columns.4.own, f32[2,512,512]{2,1,0:T(8,128)S(1)} %join_columns.5.other, f32[4,1024,1024]{2,1,0:T(8,128)} %bitcast.18, ...), custom_call_target="tpu_custom_call", output_to_operand_aliasing={{0}: (6, {})} | custom-call | flops 6442450944 | bytes 16777216 | tf_op jit(solution)/shard_map/finish_pairs/pallas_call | solution.py:241
  (117 shorter events, 31.6 us)
Async XLA Ops:
  7.2 159.9 %all-gather.3.cloned.1.call-start = ((), (), s32[]{:S(2)}) async-start(), calls=%async_computation.1 | async-start | bytes 20971520 | tf_op jit(solution)/shard_map/all_gather | solution.py:335
  9.9 35.1 %copy-start = (f32[128,4096]{1,0:T(8,128)S(1)}, f32[128,4096]{1,0:T(8,128)}, u32[]{:S(2)}) copy-start(f32[128,4096]{1,0:T(8,128)} %trailing.5) | copy-start | bytes 6291460
  43.1 6.2 %collective-permute-start = (f32[4,128,1152]{2,1,0:T(8,128)S(1)}, f32[4,128,1152]{2,1,0:T(8,128)}, u32[]{:S(2)}, u32[]{:S(2)}) collective-permute-start(f32[4,128,1152]{2,1,0:T(8,128)S(1)} %all_to_all.5.fac_own), channel_id=1, source_target_pairs={{0,4},{4,0},{1,5},{5,1},{2,6},{6,2},{3,7},{7,3},{8,12},{12,8},{9,1... | collective-permute-start | bytes 7077896 | tf_op jit(solution)/shard_map/ppermute | solution.py:53
  46.1 15.1 %collective-permute-start.6 = (f32[128,1024]{1,0:T(8,128)}, f32[128,1024]{1,0:T(8,128)S(1)}, u32[]{:S(2)}, u32[]{:S(2)}) collective-permute-start(f32[128,1024]{1,0:T(8,128)} %get-tuple-element.24), channel_id=1, source_target_pairs={{0,24},{8,16},{16,8},{24,0},{1,25},{9,17},{17,9},{25,1},{2,26},{10... | collective-permute-start | bytes 1572872 | tf_op jit(solution)/shard_map/ppermute | solution.py:60
  47.0 14.3 %collective-permute-start.5 = (f32[128,1024]{1,0:T(8,128)}, f32[128,1024]{1,0:T(8,128)}, u32[]{:S(2)}, u32[]{:S(2)}) collective-permute-start(f32[128,1024]{1,0:T(8,128)} %get-tuple-element.24), channel_id=1, source_target_pairs={{0,8},{8,0},{16,24},{24,16},{1,9},{9,1},{17,25},{25,17},{2,10},{10... | collective-permute-start | bytes 1572872 | tf_op jit(solution)/shard_map/ppermute | solution.py:60
  50.8 12.6 %collective-permute-start.1 = (f32[512,128]{1,0:T(8,128)S(1)}, f32[512,128]{1,0:T(8,128)}, u32[]{:S(2)}, u32[]{:S(2)}) collective-permute-start(f32[512,128]{1,0:T(8,128)S(1)} %solve_pair.4), channel_id=1, source_target_pairs={{96,32},{97,33},{98,34},{99,35},{100,36},{101,37},{102,38},{103,39... | collective-permute-start | bytes 786440 | tf_op jit(solution)/shard_map/ppermute | solution.py:356
  52.2 11.2 %collective-permute-start.2 = (f32[512,128]{1,0:T(8,128)S(1)}, f32[512,128]{1,0:T(8,128)}, u32[]{:S(2)}, u32[]{:S(2)}) collective-permute-start(f32[512,128]{1,0:T(8,128)S(1)} %solve_pair.4), channel_id=1, source_target_pairs={{96,64},{97,65},{98,66},{99,67},{100,68},{101,69},{102,70},{103,71... | collective-permute-start | bytes 786440 | tf_op jit(solution)/shard_map/ppermute | solution.py:356
  53.5 14.8 %collective-permute-start.3 = (f32[512,128]{1,0:T(8,128)S(1)}, f32[512,128]{1,0:T(8,128)}, u32[]{:S(2)}, u32[]{:S(2)}) collective-permute-start(f32[512,128]{1,0:T(8,128)S(1)} %solve_pair.4), channel_id=1, source_target_pairs={{96,0},{97,1},{98,2},{99,3},{100,4},{101,5},{102,6},{103,7},{104,8... | collective-permute-start | bytes 786440 | tf_op jit(solution)/shard_map/ppermute | solution.py:356
  54.8 16.8 %copy-start.1 = (f32[128,4096]{1,0:T(8,128)S(1)}, f32[128,4096]{1,0:T(8,128)}, u32[]{:S(2)}) copy-start(f32[128,4096]{1,0:T(8,128)} %trailing.5) | copy-start | bytes 6291460
  61.2 10.2 %collective-permute-start.7 = (f32[64,1024]{1,0:T(8,128)S(1)}, f32[64,1024]{1,0:T(8,128)S(1)}, u32[]{:S(2)}, u32[]{:S(2)}) collective-permute-start(f32[64,1024]{1,0:T(8,128)S(1)} %slice.54), channel_id=1, source_target_pairs={{0,8},{8,0},{16,24},{24,16},{1,9},{9,1},{17,25},{25,17},{2,10},{10... | collective-permute-start | bytes 786440 | tf_op jit(solution)/shard_map/ppermute | solution.py:65
  62.4 9.0 %collective-permute-start.8 = (f32[64,1024]{1,0:T(8,128)S(1)}, f32[64,1024]{1,0:T(8,128)S(1)}, u32[]{:S(2)}, u32[]{:S(2)}) collective-permute-start(f32[64,1024]{1,0:T(8,128)S(1)} %slice.55), channel_id=1, source_target_pairs={{0,24},{8,16},{16,8},{24,0},{1,25},{9,17},{17,9},{25,1},{2,26},{10... | collective-permute-start | bytes 786440 | tf_op jit(solution)/shard_map/ppermute | solution.py:66
  69.5 2.1 %collective-permute-start.4 = (f32[512,128]{1,0:T(8,128)S(1)}, f32[512,128]{1,0:T(8,128)S(1)}, u32[]{:S(2)}, u32[]{:S(2)}) collective-permute-start(f32[512,128]{1,0:T(8,128)S(1)} %add_select_fusion.2.mine), channel_id=1, source_target_pairs={{0,4},{4,0},{1,5},{5,1},{2,6},{6,2},{3,7},{7,3},{8,12},{12,8},{9,1... | collective-permute-start | bytes 786440 | tf_op jit(solution)/shard_map/ppermute | solution.py:53
  70.5 15.0 %collective-permute-start.15 = (f32[128,1024]{1,0:T(8,128)}, f32[128,1024]{1,0:T(8,128)}, u32[]{:S(2)}, u32[]{:S(2)}) collective-permute-start(f32[128,1024]{1,0:T(8,128)} %get-tuple-element.25), channel_id=1, source_target_pairs={{0,24},{8,16},{16,8},{24,0},{1,25},{9,17},{17,9},{25,1},{2,26},{10... | collective-permute-start | bytes 1572872 | tf_op jit(solution)/shard_map/ppermute | solution.py:60
  71.4 15.2 %collective-permute-start.14 = (f32[128,1024]{1,0:T(8,128)}, f32[128,1024]{1,0:T(8,128)}, u32[]{:S(2)}, u32[]{:S(2)}) collective-permute-start(f32[128,1024]{1,0:T(8,128)} %get-tuple-element.25), channel_id=1, source_target_pairs={{0,8},{8,0},{16,24},{24,16},{1,9},{9,1},{17,25},{25,17},{2,10},{10... | collective-permute-start | bytes 1572872 | tf_op jit(solution)/shard_map/ppermute | solution.py:60
  75.6 2.0 collective-permute-start.9
  78.2 13.8 %collective-permute-start.10 = (f32[512,128]{1,0:T(8,128)S(1)}, f32[512,128]{1,0:T(8,128)}, u32[]{:S(2)}, u32[]{:S(2)}) collective-permute-start(f32[512,128]{1,0:T(8,128)S(1)} %solve_pair.5), channel_id=1, source_target_pairs={{64,0},{65,1},{66,2},{67,3},{68,4},{69,5},{70,6},{71,7},{72,8},{73... | collective-permute-start | bytes 786440 | tf_op jit(solution)/shard_map/ppermute | solution.py:356
  79.5 12.5 %collective-permute-start.11 = (f32[512,128]{1,0:T(8,128)S(1)}, f32[512,128]{1,0:T(8,128)S(1)}, u32[]{:S(2)}, u32[]{:S(2)}) collective-permute-start(f32[512,128]{1,0:T(8,128)S(1)} %solve_pair.5), channel_id=1, source_target_pairs={{64,32},{65,33},{66,34},{67,35},{68,36},{69,37},{70,38},{71,39},{7... | collective-permute-start | bytes 786440 | tf_op jit(solution)/shard_map/ppermute | solution.py:356
  80.2 12.5 %collective-permute-start.12 = (f32[512,128]{1,0:T(8,128)S(1)}, f32[512,128]{1,0:T(8,128)}, u32[]{:S(2)}, u32[]{:S(2)}) collective-permute-start(f32[512,128]{1,0:T(8,128)S(1)} %solve_pair.5), channel_id=1, source_target_pairs={{64,96},{65,97},{66,98},{67,99},{68,100},{69,101},{70,102},{71,103... | collective-permute-start | bytes 786440 | tf_op jit(solution)/shard_map/ppermute | solution.py:356
  86.4 11.3 %collective-permute-start.16 = (f32[64,1024]{1,0:T(8,128)S(1)}, f32[64,1024]{1,0:T(8,128)S(1)}, u32[]{:S(2)}, u32[]{:S(2)}) collective-permute-start(f32[64,1024]{1,0:T(8,128)S(1)} %slice.56), channel_id=1, source_target_pairs={{0,8},{8,0},{16,24},{24,16},{1,9},{9,1},{17,25},{25,17},{2,10},{10... | collective-permute-start | bytes 786440 | tf_op jit(solution)/shard_map/ppermute | solution.py:65
  87.5 10.3 %collective-permute-start.17 = (f32[64,1024]{1,0:T(8,128)S(1)}, f32[64,1024]{1,0:T(8,128)S(1)}, u32[]{:S(2)}, u32[]{:S(2)}) collective-permute-start(f32[64,1024]{1,0:T(8,128)S(1)} %slice.57), channel_id=1, source_target_pairs={{0,24},{8,16},{16,8},{24,0},{1,25},{9,17},{17,9},{25,1},{2,26},{10... | collective-permute-start | bytes 786440 | tf_op jit(solution)/shard_map/ppermute | solution.py:66
  93.9 3.9 %collective-permute-start.13 = (f32[512,128]{1,0:T(8,128)S(1)}, f32[512,128]{1,0:T(8,128)S(1)}, u32[]{:S(2)}, u32[]{:S(2)}) collective-permute-start(f32[512,128]{1,0:T(8,128)S(1)} %add_select_fusion.1.mine), channel_id=1, source_target_pairs={{0,4},{4,0},{1,5},{5,1},{2,6},{6,2},{3,7},{7,3},{8,12},{12,8},{9,1... | collective-permute-start | bytes 786440 | tf_op jit(solution)/shard_map/ppermute | solution.py:53
  95.4 15.0 %collective-permute-start.28 = (f32[128,1024]{1,0:T(8,128)}, f32[128,1024]{1,0:T(8,128)}, u32[]{:S(2)}, u32[]{:S(2)}) collective-permute-start(f32[128,1024]{1,0:T(8,128)} %get-tuple-element.28), channel_id=1, source_target_pairs={{0,24},{8,16},{16,8},{24,0},{1,25},{9,17},{17,9},{25,1},{2,26},{10... | collective-permute-start | bytes 1572872 | tf_op jit(solution)/shard_map/ppermute | solution.py:60
  96.7 14.8 %collective-permute-start.27 = (f32[128,1024]{1,0:T(8,128)}, f32[128,1024]{1,0:T(8,128)}, u32[]{:S(2)}, u32[]{:S(2)}) collective-permute-start(f32[128,1024]{1,0:T(8,128)} %get-tuple-element.28), channel_id=1, source_target_pairs={{0,8},{8,0},{16,24},{24,16},{1,9},{9,1},{17,25},{25,17},{2,10},{10... | collective-permute-start | bytes 1572872 | tf_op jit(solution)/shard_map/ppermute | solution.py:60
  101.1 1.9 collective-permute-start.22
  103.6 17.8 %copy-start.7 = (f32[512,128]{1,0:T(8,128)}, f32[512,128]{1,0:T(8,128)S(1)}, u32[]{:S(2)}) copy-start(f32[512,128]{1,0:T(8,128)S(1)} %solve_pair.6) | copy-start | bytes 786436
  103.6 10.7 %collective-permute-start.23 = (f32[512,128]{1,0:T(8,128)S(1)}, f32[512,128]{1,0:T(8,128)}, u32[]{:S(2)}, u32[]{:S(2)}) collective-permute-start(f32[512,128]{1,0:T(8,128)S(1)} %solve_pair.6), channel_id=1, source_target_pairs={{32,96},{33,97},{34,98},{35,99},{36,100},{37,101},{38,102},{39,103... | collective-permute-start | bytes 786440 | tf_op jit(solution)/shard_map/ppermute | solution.py:356
  105.0 16.4 %collective-permute-start.24 = (f32[512,128]{1,0:T(8,128)S(1)}, f32[512,128]{1,0:T(8,128)}, u32[]{:S(2)}, u32[]{:S(2)}) collective-permute-start(f32[512,128]{1,0:T(8,128)S(1)} %solve_pair.6), channel_id=1, source_target_pairs={{32,0},{33,1},{34,2},{35,3},{36,4},{37,5},{38,6},{39,7},{40,8},{41... | collective-permute-start | bytes 786440 | tf_op jit(solution)/shard_map/ppermute | solution.py:356
  106.3 15.1 %collective-permute-start.25 = (f32[512,128]{1,0:T(8,128)S(1)}, f32[512,128]{1,0:T(8,128)}, u32[]{:S(2)}, u32[]{:S(2)}) collective-permute-start(f32[512,128]{1,0:T(8,128)S(1)} %solve_pair.6), channel_id=1, source_target_pairs={{32,64},{33,65},{34,66},{35,67},{36,68},{37,69},{38,70},{39,71},{4... | collective-permute-start | bytes 786440 | tf_op jit(solution)/shard_map/ppermute | solution.py:356
  107.6 17.9 %copy-start.3 = (f32[128,4096]{1,0:T(8,128)S(1)}, f32[128,4096]{1,0:T(8,128)}, u32[]{:S(2)}) copy-start(f32[128,4096]{1,0:T(8,128)} %trailing.5) | copy-start | bytes 6291460
  111.4 14.1 %collective-permute-start.29 = (f32[64,1024]{1,0:T(8,128)S(1)}, f32[64,1024]{1,0:T(8,128)S(1)}, u32[]{:S(2)}, u32[]{:S(2)}) collective-permute-start(f32[64,1024]{1,0:T(8,128)S(1)} %slice.60), channel_id=1, source_target_pairs={{0,8},{8,0},{16,24},{24,16},{1,9},{9,1},{17,25},{25,17},{2,10},{10... | collective-permute-start | bytes 786440 | tf_op jit(solution)/shard_map/ppermute | solution.py:65
  112.4 13.0 %collective-permute-start.30 = (f32[64,1024]{1,0:T(8,128)S(1)}, f32[64,1024]{1,0:T(8,128)S(1)}, u32[]{:S(2)}, u32[]{:S(2)}) collective-permute-start(f32[64,1024]{1,0:T(8,128)S(1)} %slice.61), channel_id=1, source_target_pairs={{0,24},{8,16},{16,8},{24,0},{1,25},{9,17},{17,9},{25,1},{2,26},{10... | collective-permute-start | bytes 786440 | tf_op jit(solution)/shard_map/ppermute | solution.py:66
  122.5 2.9 %collective-permute-start.26 = (f32[512,128]{1,0:T(8,128)S(1)}, f32[512,128]{1,0:T(8,128)S(1)}, u32[]{:S(2)}, u32[]{:S(2)}) collective-permute-start(f32[512,128]{1,0:T(8,128)S(1)} %add_select_fusion.mine), channel_id=1, source_target_pairs={{0,4},{4,0},{1,5},{5,1},{2,6},{6,2},{3,7},{7,3},{8,12},{12,8},{9,1... | collective-permute-start | bytes 786440 | tf_op jit(solution)/shard_map/ppermute | solution.py:53
  124.3 15.1 %collective-permute-start.19 = (f32[2,512,128]{2,1,0:T(8,128)}, f32[2,512,128]{2,1,0:T(8,128)S(1)}, u32[]{:S(2)}, u32[]{:S(2)}) collective-permute-start(f32[2,512,128]{2,1,0:T(8,128)} %pad_maximum_fusion.2.refs_0_), channel_id=1, source_target_pairs={{0,24},{8,16},{16,8},{24,0},{1,25},{9,17},{17,9},{25,1},{2,26},{10... | collective-permute-start | bytes 1572872 | tf_op jit(solution)/shard_map/ppermute | solution.py:60
  125.2 14.4 %collective-permute-start.18 = (f32[2,512,128]{2,1,0:T(8,128)}, f32[2,512,128]{2,1,0:T(8,128)}, u32[]{:S(2)}, u32[]{:S(2)}) collective-permute-start(f32[2,512,128]{2,1,0:T(8,128)} %pad_maximum_fusion.2.refs_0_), channel_id=1, source_target_pairs={{0,8},{8,0},{16,24},{24,16},{1,9},{9,1},{17,25},{25,17},{2,10},{10... | collective-permute-start | bytes 1572872 | tf_op jit(solution)/shard_map/ppermute | solution.py:60
  128.6 1.8 collective-permute-start.31
  134.4 8.1 %collective-permute-start.32 = (f32[512,128]{1,0:T(8,128)S(1)}, f32[512,128]{1,0:T(8,128)S(1)}, u32[]{:S(2)}, u32[]{:S(2)}) collective-permute-start(f32[512,128]{1,0:T(8,128)S(1)} %solve_pair.7), channel_id=1, source_target_pairs={{0,64},{1,65},{2,66},{3,67},{4,68},{5,69},{6,70},{7,71},{8,72},{9,... | collective-permute-start | bytes 786440 | tf_op jit(solution)/shard_map/ppermute | solution.py:356
  135.7 6.9 %collective-permute-start.33 = (f32[512,128]{1,0:T(8,128)S(1)}, f32[512,128]{1,0:T(8,128)S(1)}, u32[]{:S(2)}, u32[]{:S(2)}) collective-permute-start(f32[512,128]{1,0:T(8,128)S(1)} %solve_pair.7), channel_id=1, source_target_pairs={{0,96},{1,97},{2,98},{3,99},{4,100},{5,101},{6,102},{7,103},{8,104... | collective-permute-start | bytes 786440 | tf_op jit(solution)/shard_map/ppermute | solution.py:356
  137.0 9.9 %collective-permute-start.34 = (f32[512,128]{1,0:T(8,128)S(1)}, f32[512,128]{1,0:T(8,128)S(1)}, u32[]{:S(2)}, u32[]{:S(2)}) collective-permute-start(f32[512,128]{1,0:T(8,128)S(1)} %solve_pair.7), channel_id=1, source_target_pairs={{0,32},{1,33},{2,34},{3,35},{4,36},{5,37},{6,38},{7,39},{8,40},{9,... | collective-permute-start | bytes 786440 | tf_op jit(solution)/shard_map/ppermute | solution.py:356
  139.4 7.6 %collective-permute-start.20 = (f32[2,256,128]{2,1,0:T(8,128)S(1)}, f32[2,256,128]{2,1,0:T(8,128)S(1)}, u32[]{:S(2)}, u32[]{:S(2)}) collective-permute-start(f32[2,256,128]{2,1,0:T(8,128)S(1)} %slice.58), channel_id=1, source_target_pairs={{0,8},{8,0},{16,24},{24,16},{1,9},{9,1},{17,25},{25,17},{2,10},{10... | collective-permute-start | bytes 786440 | tf_op jit(solution)/shard_map/ppermute | solution.py:65
  140.6 8.6 %collective-permute-start.21 = (f32[2,256,128]{2,1,0:T(8,128)S(1)}, f32[2,256,128]{2,1,0:T(8,128)S(1)}, u32[]{:S(2)}, u32[]{:S(2)}) collective-permute-start(f32[2,256,128]{2,1,0:T(8,128)S(1)} %slice.59), channel_id=1, source_target_pairs={{0,24},{8,16},{16,8},{24,0},{1,25},{9,17},{17,9},{25,1},{2,26},{10... | collective-permute-start | bytes 786440 | tf_op jit(solution)/shard_map/ppermute | solution.py:66
  151.0 6.4 %collective-permute-start.38 = (f32[2,512,512]{2,1,0:T(8,128)S(1)}, f32[2,512,512]{2,1,0:T(8,128)}, u32[]{:S(2)}, u32[]{:S(2)}) collective-permute-start(f32[2,512,512]{2,1,0:T(8,128)S(1)} %join_columns.3.own), channel_id=1, source_target_pairs={{0,4},{4,0},{1,5},{5,1},{2,6},{6,2},{3,7},{7,3},{8,12},{12,8},{9,1... | collective-permute-start | bytes 6291464 | tf_op jit(solution)/shard_map/ppermute | solution.py:53
  153.2 24.9 %collective-permute-start.35 = (f32[2,512,128]{2,1,0:T(8,128)S(1)}, f32[2,512,128]{2,1,0:T(8,128)}, u32[]{:S(2)}, u32[]{:S(2)}) collective-permute-start(f32[2,512,128]{2,1,0:T(8,128)S(1)} %pad_maximum_fusion.3.refs_0_), channel_id=1, source_target_pairs={{0,8},{8,0},{16,24},{24,16},{1,9},{9,1},{17,25},{25,17},{2,10},{10... | collective-permute-start | bytes 1572872 | tf_op jit(solution)/shard_map/ppermute | solution.py:368
  153.4 24.7 %collective-permute-start.36 = (f32[2,512,128]{2,1,0:T(8,128)S(1)}, f32[2,512,128]{2,1,0:T(8,128)}, u32[]{:S(2)}, u32[]{:S(2)}) collective-permute-start(f32[2,512,128]{2,1,0:T(8,128)S(1)} %pad_maximum_fusion.3.refs_0_), channel_id=1, source_target_pairs={{0,24},{8,16},{16,8},{24,0},{1,25},{9,17},{17,9},{25,1},{2,26},{10... | collective-permute-start | bytes 1572872 | tf_op jit(solution)/shard_map/ppermute | solution.py:368
  155.2 24.5 %collective-permute-start.37 = (f32[2,512,128]{2,1,0:T(8,128)S(1)}, f32[2,512,128]{2,1,0:T(8,128)}, u32[]{:S(2)}, u32[]{:S(2)}) collective-permute-start(f32[2,512,128]{2,1,0:T(8,128)S(1)} %pad_maximum_fusion.3.refs_0_), channel_id=1, source_target_pairs={{0,16},{8,24},{16,0},{24,8},{1,17},{9,25},{17,1},{25,9},{2,18},{10... | collective-permute-start | bytes 1572872 | tf_op jit(solution)/shard_map/ppermute | solution.py:368
  156.5 26.5 %collective-permute-start.39 = (f32[2,512,128]{2,1,0:T(8,128)S(1)}, f32[2,512,128]{2,1,0:T(8,128)S(1)}, u32[]{:S(2)}, u32[]{:S(2)}) collective-permute-start(f32[2,512,128]{2,1,0:T(8,128)S(1)} %pad_maximum_fusion.3.refs_0_), channel_id=1, source_target_pairs={{0,4},{4,0},{1,5},{5,1},{2,6},{6,2},{3,7},{7,3},{8,12},{12,8},{9,1... | collective-permute-start | bytes 1572872 | tf_op jit(solution)/shard_map/ppermute | solution.py:53
  179.7 3.4 %collective-permute-start.40 = (f32[2,512,128]{2,1,0:T(8,128)}, f32[2,512,128]{2,1,0:T(8,128)S(1)}, u32[]{:S(2)}, u32[]{:S(2)}) collective-permute-start(f32[2,512,128]{2,1,0:T(8,128)} %collective-permute-done.35.refs_1_), channel_id=1, source_target_pairs={{0,4},{4,0},{1,5},{5,1},{2,6},{6,2},{3,7},{7,3},{8,12},{12,8},{9,1... | collective-permute-start | bytes 1572872 | tf_op jit(solution)/shard_map/ppermute | solution.py:53
  180.5 2.6 %collective-permute-start.41 = (f32[2,512,128]{2,1,0:T(8,128)}, f32[2,512,128]{2,1,0:T(8,128)S(1)}, u32[]{:S(2)}, u32[]{:S(2)}) collective-permute-start(f32[2,512,128]{2,1,0:T(8,128)} %collective-permute-done.36.refs_2_), channel_id=1, source_target_pairs={{0,4},{4,0},{1,5},{5,1},{2,6},{6,2},{3,7},{7,3},{8,12},{12,8},{9,1... | collective-permute-start | bytes 1572872 | tf_op jit(solution)/shard_map/ppermute | solution.py:53
  180.5 3.2 %collective-permute-start.42 = (f32[2,512,128]{2,1,0:T(8,128)}, f32[2,512,128]{2,1,0:T(8,128)S(1)}, u32[]{:S(2)}, u32[]{:S(2)}) collective-permute-start(f32[2,512,128]{2,1,0:T(8,128)} %collective-permute-done.37.refs_3_), channel_id=1, source_target_pairs={{0,4},{4,0},{1,5},{5,1},{2,6},{6,2},{3,7},{7,3},{8,12},{12,8},{9,1... | collective-permute-start | bytes 1572872 | tf_op jit(solution)/shard_map/ppermute | solution.py:53
  (9 other events, 39.9 us)
Sparse Core Ops, SparseCore 0:
  9.7 157.3 all-gather.2
